TPU v7x, 32 devices: a whole 2x2x4 slice. The times are simulated.
32 devices in a mesh: groups: 2 (over y), ep: 4 (over z), tp: 4 (over x, core).
Axes of the slice: x: 2, y: 2, z: 4, core: 2. Of those that a mesh axis runs over, the one named last changes fastest.
Arguments:
- tokens: bfloat16 [128, 2, 8192], P(('groups', 'ep')), parts along dimension 0, may hold values from -400 to 400
- query_weight: bfloat16 [8192, 8192], P('ep', 'tp'), may hold values from -0.0625 to 0.0625
- key_weight: bfloat16 [8192, 1024], P('ep', 'tp'), may hold values from -0.0625 to 0.0625
- value_weight: bfloat16 [8192, 1024], P('ep', 'tp'), may hold values from -0.0625 to 0.0625
- output_weight: bfloat16 [8192, 8192], P('tp', 'ep'), may hold values from -0.0625 to 0.0625
- adapter_down_maps: bfloat16 [32, 8192, 64], P('ep', 'tp'), may hold values from -0.0625 to 0.0625
- adapter_up_maps: bfloat16 [32, 64, 8192], P('ep', None, 'tp'), may hold values from -0.75 to 0.75
- rotated_cache_keys: bfloat16 [128, 128, 1024], P(('groups', 'ep'), None, 'tp'), parts along dimension 0, may hold values from -68 to 68
- cached_value_rows: bfloat16 [128, 128, 1024], P(('groups', 'ep'), None, 'tp'), parts along dimension 0, may hold values from -12 to 12
- adapter_index: int32 [128], P(('groups', 'ep')), parts along dimension 0, may hold values from 0 to 31, as said below
- cached_lengths: int32 [128], P(('groups', 'ep')), parts along dimension 0, may hold values from 1 to 128, as said below
Outputs:
- attn_out: bfloat16 [128, 2, 8192], P(('groups', 'ep')), parts along dimension 0
There are 2 independent parts, one for each index of `groups`. A program takes and returns all parts, laid end to end along the dimension named above; an argument that names none is the same for every part. Nothing has to cross between parts.
Inputs may be any that keep to these rules, and one draw needn't show every extreme that they name: `adapter_index`: adapters a * 8 to a * 8 + 7 belong to owner a. In each aligned block of 16 requests at most 8 requests name adapters of one owner, and one owner, the same in every block, is named by exactly 8 requests of every block. `cached_lengths`: some request has 128 cached positions.
All inputs are finite; a program needn't handle non-finite values.
Results may differ from a plain program's by a relative error of at most 0.012.
The roundings to bfloat16 on the way count: a program that leaves them out, or rounds other values in their place, can miss the bound.
Values may be sent and summed in bfloat16 or wider, within the bound.
A program may use at most 128 MiB of HBM per device.

v0:
```python
import math

import jax
import jax.numpy as jnp
from jax import lax
from jax.sharding import PartitionSpec as P

QUERY_HEADS = 64
KEY_HEADS = 8
HEAD_SIZE = 128


EPSILON = 1e-05
THETA = 500000.0
MASKED = -1e30


def normalize(tokens):
    widened = tokens.astype(jnp.float32)
    factor = lax.rsqrt(jnp.mean(widened * widened, axis=-1, keepdims=True) + EPSILON)
    return (widened * factor).astype(jnp.bfloat16)


def apply_rotation(values, token_positions):
    half_size = values.shape[-1] // 2
    pair_ranks = jnp.arange(half_size).astype(jnp.float32)
    inverse = jnp.exp(pair_ranks * (-2.0 / values.shape[-1]) * math.log(THETA))
    angles = token_positions[..., None, None] * inverse
    cosine = jnp.cos(angles)
    sine_part = jnp.sin(angles)
    lower_half = values[..., :half_size]
    upper_half = values[..., half_size:]
    return jnp.concatenate(
        [
            lower_half * cosine - upper_half * sine_part,
            upper_half * cosine + lower_half * sine_part,
        ],
        axis=-1,
    )


def attend_step(query_rows, keys_cached, values_cached, incoming_keys, incoming_values, lengths):
    score_scale = 1.0 / math.sqrt(query_rows.shape[-1])
    decode_steps = query_rows.shape[1]
    cache_len = keys_cached.shape[1]
    cached = (
        jnp.einsum("rsgmd,rcgd->rsgmc", query_rows, keys_cached, preferred_element_type=jnp.float32)
        * score_scale
    )
    fresh_scores = (
        jnp.einsum(
            "rsgmd,rtgd->rsgmt", query_rows, incoming_keys, preferred_element_type=jnp.float32
        )
        * score_scale
    )
    live_cache = (jnp.arange(cache_len)[None, :] < lengths[:, None])[:, None, None, None, :]
    live_fresh = (jnp.arange(decode_steps)[None, :] <= jnp.arange(decode_steps)[:, None])[
        None, :, None, None, :
    ]
    cached = jnp.where(live_cache, cached, MASKED)
    fresh_scores = jnp.where(live_fresh, fresh_scores, MASKED)
    row_max = jnp.maximum(
        jnp.max(cached, -1, keepdims=True), jnp.max(fresh_scores, -1, keepdims=True)
    )
    cached_exp = jnp.where(live_cache, jnp.exp(cached - row_max), 0.0)
    fresh_exp = jnp.where(live_fresh, jnp.exp(fresh_scores - row_max), 0.0)
    totals = jnp.sum(cached_exp, -1, keepdims=True) + jnp.sum(fresh_exp, -1, keepdims=True)
    cached_weight = (cached_exp / totals).astype(jnp.bfloat16)
    fresh_weight = (fresh_exp / totals).astype(jnp.bfloat16)
    mixture = jnp.einsum(
        "rsgmc,rcgd->rsgmd", cached_weight, values_cached, preferred_element_type=jnp.float32
    )
    mixture = mixture + jnp.einsum(
        "rsgmt,rtgd->rsgmd", fresh_weight, incoming_values, preferred_element_type=jnp.float32
    )
    return mixture.astype(jnp.bfloat16).reshape(query_rows.shape[0], decode_steps, -1)


def local(
    tokens,
    query_weight,
    key_weight,
    value_weight,
    output_weight,
    adapter_down_maps,
    adapter_up_maps,
    rotated_cache_keys,
    cached_value_rows,
    adapter_index,
    cached_lengths,
):
    request_batch, decode_steps, model_width = tokens.shape
    owner_count = lax.axis_size("ep")
    query_columns = query_weight.shape[1]
    key_columns = key_weight.shape[1]
    key_value_local = key_columns // HEAD_SIZE
    adapters_owned = adapter_down_maps.shape[0]
    column_portion = adapter_down_maps.shape[1]
    normed = normalize(tokens)
    capacity = max(2, (2 * request_batch + owner_count - 1) // owner_count)
    slot_count = owner_count * capacity
    owner_of = adapter_index // adapters_owned
    local_of = adapter_index % adapters_owned
    position = jnp.arange(request_batch)
    earlier = (owner_of[None, :] == owner_of[:, None]) & (position[None, :] < position[:, None])
    rank_within = jnp.sum(earlier.astype(jnp.int32), axis=1)
    slot_index = owner_of * capacity + rank_within
    placing = (jnp.arange(slot_count)[:, None] == slot_index[None, :]).astype(jnp.bfloat16)
    own_columns = lax.dynamic_slice_in_dim(
        normed, lax.axis_index("tp") * column_portion, column_portion, 2
    )
    outgoing = jnp.dot(
        placing, own_columns.reshape(request_batch, -1), preferred_element_type=jnp.float32
    )
    outgoing = outgoing.astype(jnp.bfloat16).reshape(
        owner_count, capacity, decode_steps, column_portion
    )
    label_pair = jnp.stack([local_of, position], axis=1).astype(jnp.bfloat16)
    labels = jnp.dot(placing, label_pair, preferred_element_type=jnp.float32)
    labels = labels.astype(jnp.bfloat16).reshape(owner_count, capacity, 2)
    arrived_rows = lax.all_to_all(outgoing, "ep", split_axis=0, concat_axis=0, tiled=True)
    arrived_labels = lax.all_to_all(labels, "ep", split_axis=0, concat_axis=0, tiled=True)
    selected_rows = arrived_labels[..., 0].astype(jnp.int32)
    selected_down = jnp.take(adapter_down_maps, selected_rows, axis=0)
    shrunk = jnp.einsum(
        "ocsd,ocdr->ocsr", arrived_rows, selected_down, preferred_element_type=jnp.float32
    )
    shrunk = lax.psum(shrunk, "tp").astype(jnp.bfloat16)
    selected_up = jnp.take(adapter_up_maps, selected_rows, axis=0)
    correction = jnp.einsum(
        "ocsr,ocrf->ocsf", shrunk, selected_up, preferred_element_type=jnp.float32
    ).astype(jnp.bfloat16)
    returned = lax.all_to_all(correction, "ep", split_axis=0, concat_axis=0, tiled=True)
    gathered = lax.all_to_all(normed, "ep", split_axis=2, concat_axis=0, tiled=True)
    row_count = lax.axis_size("ep") * request_batch
    row_block = gathered.reshape(row_count * decode_steps, -1)
    query_part = jnp.dot(row_block, query_weight, preferred_element_type=jnp.float32)
    key_part = jnp.dot(row_block, key_weight, preferred_element_type=jnp.float32)
    value_part = jnp.dot(row_block, value_weight, preferred_element_type=jnp.float32)
    projected_rows = lax.psum_scatter(
        jnp.concatenate([query_part, key_part, value_part], axis=1).reshape(
            row_count, decode_steps, -1
        ),
        "ep",
        scatter_dimension=0,
        tiled=True,
    )
    adapter_delta = jnp.einsum(
        "pr,pf->rf", placing, returned.reshape(slot_count, -1), preferred_element_type=jnp.float32
    )
    query_sum = projected_rows[..., :query_columns] + adapter_delta.reshape(
        request_batch, decode_steps, query_columns
    )
    token_positions = (
        cached_lengths.astype(jnp.float32)[:, None]
        + jnp.arange(decode_steps).astype(jnp.float32)[None, :]
    )
    query_rows = apply_rotation(
        query_sum.reshape(request_batch, decode_steps, -1, HEAD_SIZE), token_positions
    ).astype(jnp.bfloat16)
    incoming_keys = apply_rotation(
        projected_rows[..., query_columns : query_columns + key_columns].reshape(
            request_batch, decode_steps, key_value_local, HEAD_SIZE
        ),
        token_positions,
    ).astype(jnp.bfloat16)
    incoming_values = (
        projected_rows[..., query_columns + key_columns :]
        .astype(jnp.bfloat16)
        .reshape(request_batch, decode_steps, key_value_local, HEAD_SIZE)
    )
    query_rows = query_rows.reshape(
        request_batch, decode_steps, key_value_local, QUERY_HEADS // KEY_HEADS, HEAD_SIZE
    )
    attention_result = attend_step(
        query_rows,
        rotated_cache_keys.reshape(request_batch, -1, key_value_local, HEAD_SIZE),
        cached_value_rows.reshape(request_batch, -1, key_value_local, HEAD_SIZE),
        incoming_keys,
        incoming_values,
        cached_lengths,
    )
    gathered_piece = lax.all_gather(attention_result, "ep", axis=0, tiled=True)
    row_count = gathered_piece.shape[0]
    product = jnp.dot(
        gathered_piece.reshape(row_count * decode_steps, -1),
        output_weight,
        preferred_element_type=jnp.float32,
    )
    partial_out = product.reshape(row_count, decode_steps, -1)
    share_part = lax.psum_scatter(partial_out, "tp", scatter_dimension=2, tiled=True).astype(
        jnp.bfloat16
    )
    share_part = share_part.reshape(share_part.shape[0], decode_steps, 1, -1)
    arranged = lax.all_to_all(share_part, "ep", split_axis=0, concat_axis=2, tiled=True)
    whole_rows = lax.all_gather(arranged, "tp", axis=3, tiled=True)
    return whole_rows.reshape(request_batch, decode_steps, model_width)


def solution(mesh):
    return jax.shard_map(
        local,
        mesh=mesh,
        in_specs=(
            P(("groups", "ep"), None, None),
            P("ep", "tp"),
            P("ep", "tp"),
            P("ep", "tp"),
            P("tp", "ep"),
            P("ep", "tp", None),
            P("ep", None, "tp"),
            P(("groups", "ep"), None, "tp"),
            P(("groups", "ep"), None, "tp"),
            P(("groups", "ep")),
            P(("groups", "ep")),
        ),
        out_specs=P(("groups", "ep"), None, None),
        check_vma=False,
    )
```

profile of v0, /device:TPU:0, one launch (start us, length us, event | category | flops | bytes accessed | tf_op | source)
XLA Modules:
  0.0 208.0 jit_solution(15546309706993629568)
XLA Ops:
  6.5 1.8 fusion.19
  8.4 1.3 fusion.20
  9.7 6.7 %copy.119 = bf16[16,2,8192]{0,1,2:T(2,128)(2,1)} copy(bf16[16,2,8192]{2,0,1:T(8,128)(2,1)S(1)} %fusion.20) | data formatting | bytes 1048576 | tf_op jit(solution)/shard_map/convert_element_type | solution.py:21
  16.4 6.5 %reshape.205 = bf16[4,2,32768]{2,1,0:T(2,128)(2,1)} reshape(bf16[8192,2,16]{2,1,0:T(2,128)(2,1)} %bitcast.96) | data formatting | bytes 1048576
  22.9 6.3 %all-to-all-start = ((bf16[4,2,32768]{2,1,0:T(2,128)(2,1)}), bf16[4,2,32768]{2,1,0:T(2,128)(2,1)S(1)}, u32[]{:S(2)}, u32[]{:S(2)}) async-start(bf16[4,2,32768]{2,1,0:T(2,128)(2,1)} %reshape.205), calls=%async_computation | async-start | bytes 1048576 | tf_op jit(solution)/shard_map/all_to_all | solution.py:134
  29.3 0.2 convert_reduce_fusion
  29.5 0.3 convolution_convert_fusion
  29.8 1.0 copy.123
  30.8 0.2 convolution_convert_fusion.1
  31.1 0.6 copy.124
  31.7 12.0 %all-to-all-done = bf16[4,2,32768]{2,1,0:T(2,128)(2,1)S(1)} async-done(((bf16[4,2,32768]{2,1,0:T(2,128)(2,1)}), bf16[4,2,32768]{2,1,0:T(2,128)(2,1)S(1)}, u32[]{:S(2)}, u32[]{:S(2)}) %all-to-all-start) | async-done | bytes 524320 | tf_op jit(solution)/shard_map/all_to_all | solution.py:134
  43.7 3.2 %all-to-all-start.2 = ((bf16[4,8,2]{1,2,0:T(2,128)(2,1)}), bf16[4,8,2]{1,2,0:T(2,128)(2,1)S(1)}, u32[]{:S(2)}, u32[]{:S(2)}) async-start(bf16[4,8,2]{1,2,0:T(2,128)(2,1)} %copy.124), calls=%async_computation.3 | async-start | bytes 4096 | tf_op jit(solution)/shard_map/all_to_all | solution.py:122
  46.9 4.1 %reshape.206 = bf16[8192,2,16]{2,1,0:T(2,128)(2,1)} reshape(bf16[4,2,32768]{2,1,0:T(2,128)(2,1)S(1)} %all-to-all-done) | data formatting | bytes 1048576
  51.1 9.6 %copy.120 = bf16[16,2,4,2048]{3,1,0,2:T(2,128)(2,1)S(1)} copy(bf16[16,2,4,2048]{0,1,3,2:T(2,128)(2,1)} %bitcast.95) | data formatting | bytes 1048576 | tf_op jit(solution)/shard_map/all_to_all | solution.py:134
  60.7 0.2 reshape.158
  60.9 4.8 %fusion.60 = f32[128,2048]{1,0:T(8,128)S(1)} fusion(bf16[128,2048]{1,0:T(8,128)(2,1)S(1)} %reshape.158, bf16[2048,2048]{1,0:T(8,128)(2,1)} %param.12), kind=kOutput, calls=%fused_computation.107 | convolution fusion | flops 1073741824 | bytes 9961472 | tf_op jit(solution)/shard_map/dot_general | solution.py:137
  65.7 0.3 fusion.61
  66.0 0.3 fusion.62
  66.5 1.8 reshape.159
  68.3 2.6 %copy.121 = f32[64,2,2560]{2,0,1:T(8,128)} copy(f32[64,2,2560]{2,1,0:T(2,128)} %reshape.159) | data formatting | bytes 2621440 | tf_op jit(solution)/shard_map/reshape | solution.py:141
  71.1 1.3 reshape.165
  72.4 2.2 %reshape.167 = bf16[16,128,2,128]{3,2,1,0:T(2,128)(2,1)} reshape(bf16[16,128,256]{2,1,0:T(8,128)(2,1)} %param.19) | data formatting | bytes 2097152 | tf_op jit(solution)/shard_map/reshape | solution.py:178
  74.6 5.0 %all-to-all-start.1 = ((bf16[4,8,2,2048]{3,2,1,0:T(2,128)(2,1)}), bf16[4,8,2,2048]{3,2,1,0:T(2,128)(2,1)S(1)}, u32[]{:S(2)}, u32[]{:S(2)}) async-start(bf16[4,8,2,2048]{3,2,1,0:T(2,128)(2,1)} %copy.123), calls=%async_computation.2 | async-start | bytes 524288 | tf_op jit(solution)/shard_map/all_to_all | solution.py:121
  79.7 4.9 %gather_fusion = bf16[32,2048,64]{1,2,0:T(8,128)(2,1)} fusion(bf16[8,2048,64]{1,2,0:T(8,128)(2,1)S(1)} %copy-done, s32[1024]{0:T(1024)S(1)} %pad_clamp_fusion), kind=kCustom, calls=%fused_computation | custom fusion | bytes 16777344 | tf_op jit(solution)/shard_map/jit(_take)/gather | solution.py:124
  84.6 6.5 %gather_fusion.1 = bf16[32,64,2048]{2,1,0:T(8,128)(2,1)} fusion(bf16[8,64,2048]{2,1,0:T(8,128)(2,1)} %param.17, s32[1024]{0:T(1024)S(1)} %pad_clamp_fusion), kind=kCustom, calls=%fused_computation.1 | custom fusion | bytes 16777344 | tf_op jit(solution)/shard_map/jit(_take)/gather | solution.py:129
  91.1 4.1 %all-to-all-done.1 = bf16[4,8,2,2048]{3,2,1,0:T(2,128)(2,1)S(1)} async-done(((bf16[4,8,2,2048]{3,2,1,0:T(2,128)(2,1)}), bf16[4,8,2,2048]{3,2,1,0:T(2,128)(2,1)S(1)}, u32[]{:S(2)}, u32[]{:S(2)}) %all-to-all-start.1) | async-done | bytes 262176 | tf_op jit(solution)/shard_map/all_to_all | solution.py:121
  95.2 5.8 %fusion.4 = f32[4,8,2,64]{3,2,1,0:T(2,128)S(1)} fusion(bf16[4,8,2,2048]{3,2,1,0:T(2,128)(2,1)S(1)} %all-to-all-done.1, bf16[4,8,2048,64]{2,3,1,0:T(8,128)(2,1)} %bitcast.94, pred[4,8]{1,0:T(4,128)(4,1)S(1)} %bitcast.107), kind=kOutput, calls=%fused_computation.6 | convolution fusion | flops 20971520 | bytes 8667168 | tf_op jit(solution)/shard_map/ocsd,ocdr->ocsr/dot_general | solution.py:125
  101.0 10.9 %psum.7 = bf16[4,8,2,64]{3,2,1,0:T(2,128)(2,1)S(1)} all-reduce(f32[4,8,2,64]{3,2,1,0:T(2,128)S(1)} %fusion.4), channel_id=1, replica_groups=mesh['groups'=2,'ep'=4,'tp'=4] {'tp'}, use_global_device_ids=true, to_apply=%region_3.4 | all-reduce | flops 4096 | bytes 24576 | tf_op jit(solution)/shard_map/psum | solution.py:128
  111.8 5.6 %fusion.10 = bf16[4,8,2,2048]{3,2,1,0:T(2,128)(2,1)} fusion(bf16[4,8,64,2048]{3,2,1,0:T(8,128)(2,1)} %bitcast.97, pred[4,8]{1,0:T(4,128)(4,1)S(1)} %bitcast.108, bf16[4,8,2,64]{3,2,1,0:T(2,128)(2,1)S(1)} %psum.7), kind=kOutput, calls=%fused_computation.13 | convolution fusion | flops 21102592 | bytes 8658976 | tf_op jit(solution)/shard_map/ocsr,ocrf->ocsf/dot_general | solution.py:130
  117.4 3.8 %all-to-all-start.3 = ((bf16[4,8,2,2048]{3,2,1,0:T(2,128)(2,1)}), bf16[4,8,2,2048]{3,2,1,0:T(2,128)(2,1)S(1)}, u32[]{:S(2)}, u32[]{:S(2)}) async-start(bf16[4,8,2,2048]{3,2,1,0:T(2,128)(2,1)} %fusion.10), calls=%async_computation.4 | async-start | bytes 524288 | tf_op jit(solution)/shard_map/all_to_all | solution.py:133
  121.3 0.3 multiply_cosine_fusion
  121.6 8.8 %all-to-all-done.3 = bf16[4,8,2,2048]{3,2,1,0:T(2,128)(2,1)S(1)} async-done(((bf16[4,8,2,2048]{3,2,1,0:T(2,128)(2,1)}), bf16[4,8,2,2048]{3,2,1,0:T(2,128)(2,1)S(1)}, u32[]{:S(2)}, u32[]{:S(2)}) %all-to-all-start.3) | async-done | bytes 262176 | tf_op jit(solution)/shard_map/all_to_all | solution.py:133
  130.4 1.2 convolution_add_fusion
  131.8 0.8 slice.41
  132.8 0.8 fusion.58
  133.6 0.8 fusion.59
  134.6 0.3 fusion.25
  134.9 0.8 slice.54
  135.7 0.3 convolution_bitcast_fusion.1
  136.0 0.4 fusion.16
  136.6 16.3 %all_gather.6 = bf16[64,2,2048]{2,0,1:T(8,128)(2,1)S(1)} all-gather(bf16[16,2,2048]{2,0,1:T(8,128)(2,1)S(1)} %reshape.169), channel_id=1, replica_groups=mesh['groups'=2,'ep'=4,'tp'=4] {'ep'}, dimensions={0}, use_global_device_ids=true | all-gather | bytes 655360 | tf_op jit(solution)/shard_map/all_gather | solution.py:183
  152.9 5.7 %fusion = f32[64,2,2048]{2,0,1:T(8,128)} fusion(bf16[64,2,2048]{2,0,1:T(8,128)(2,1)S(1)} %all_gather.6, bf16[2048,2048]{1,0:T(8,128)(2,1)} %param.15), kind=kOutput, calls=%fused_computation.2 | convolution fusion | flops 1073741824 | bytes 9961472 | tf_op jit(solution)/shard_map/dot_general | solution.py:185
  158.6 22.8 %reduce-scatter.5.cloned.1.call-done = f32[64,2,512]{2,0,1:T(8,128)} async-done(((f32[64,2,2048]{2,0,1:T(8,128)}), f32[64,2,512]{2,0,1:T(8,128)}) %reduce-scatter.5.cloned.1.call-update) | async-done | bytes 262160 | tf_op jit(solution)/shard_map/reduce_scatter | solution.py:191
  181.3 1.0 convert_bitcast_fusion
  182.4 10.5 %all_to_all.48 = bf16[64,2,1,512]{3,1,2,0:T(2,128)(2,1)S(1)} all-to-all(bf16[64,2,1,512]{3,1,2,0:T(2,128)(2,1)S(1)} %copy.137), channel_id=1, replica_groups=mesh['groups'=2,'ep'=4,'tp'=4] {'ep'}, dimensions={0} | all-to-all | bytes 262144 | tf_op jit(solution)/shard_map/all_to_all | solution.py:195
  192.9 6.5 %all-gather = bf16[16,2,4,1,2048]{4,1,0,2,3:T(2,128)(2,1)S(1)} all-gather(bf16[16,2,4,1,512]{4,1,0,2,3:T(2,128)(2,1)S(1)} %bitcast.104), channel_id=2, replica_groups=mesh['groups'=2,'ep'=4,'tp'=4] {'tp'}, dimensions={4}, use_global_device_ids=true | all-gather | bytes 655360 | tf_op jit(solution)/shard_map/all_gather | solution.py:196
  199.4 0.4 copy.138
  199.8 1.3 reshape.171
  (52 shorter events, 1.5 us)
Async XLA Ops:
  6.5 73.2 %copy-start = (bf16[8,2048,64]{1,2,0:T(8,128)(2,1)S(1)}, bf16[8,2048,64]{1,2,0:T(8,128)(2,1)}, u32[]{:S(2)}) copy-start(bf16[8,2048,64]{1,2,0:T(8,128)(2,1)} %param.16) | copy-start | bytes 6291460
  6.5 22.7 %copy-start.6 = (s32[16]{0:T(128)S(1)}, s32[16]{0:T(128)}, u32[]{:S(2)}) copy-start(s32[16]{0:T(128)} %param.20) | copy-start | bytes 196
  6.5 25.1 %copy-start.5 = (s32[16]{0:T(128)S(1)}, s32[16]{0:T(128)}, u32[]{:S(2)}) copy-start(s32[16]{0:T(128)} %param.21) | copy-start | bytes 196
  22.9 20.8 %all-to-all-start = ((bf16[4,2,32768]{2,1,0:T(2,128)(2,1)}), bf16[4,2,32768]{2,1,0:T(2,128)(2,1)S(1)}, u32[]{:S(2)}, u32[]{:S(2)}) async-start(bf16[4,2,32768]{2,1,0:T(2,128)(2,1)} %reshape.205), calls=%async_computation | async-start | bytes 1048576 | tf_op jit(solution)/shard_map/all_to_all | solution.py:134
  43.7 30.9 %all-to-all-start.2 = ((bf16[4,8,2]{1,2,0:T(2,128)(2,1)}), bf16[4,8,2]{1,2,0:T(2,128)(2,1)S(1)}, u32[]{:S(2)}, u32[]{:S(2)}) async-start(bf16[4,8,2]{1,2,0:T(2,128)(2,1)} %copy.124), calls=%async_computation.3 | async-start | bytes 4096 | tf_op jit(solution)/shard_map/all_to_all | solution.py:122
  46.9 83.5 %reduce-scatter.3.cloned.1.call-start = ((), (), s32[]{:S(2)}) async-start(), calls=%async_computation.7 | async-start | bytes 1638400 | tf_op jit(solution)/shard_map/reduce_scatter | solution.py:140
  60.9 4.8 %copy-start.3 = (bf16[2048,256]{1,0:T(8,128)(2,1)S(1)}, bf16[2048,256]{1,0:T(8,128)(2,1)}, u32[]{:S(2)}) copy-start(bf16[2048,256]{1,0:T(8,128)(2,1)} %param.13) | copy-start | bytes 3145732
  60.9 5.1 %copy-start.4 = (bf16[2048,256]{1,0:T(8,128)(2,1)S(1)}, bf16[2048,256]{1,0:T(8,128)(2,1)}, u32[]{:S(2)}) copy-start(bf16[2048,256]{1,0:T(8,128)(2,1)} %param.14) | copy-start | bytes 3145732
  74.6 20.6 %all-to-all-start.1 = ((bf16[4,8,2,2048]{3,2,1,0:T(2,128)(2,1)}), bf16[4,8,2,2048]{3,2,1,0:T(2,128)(2,1)S(1)}, u32[]{:S(2)}, u32[]{:S(2)}) async-start(bf16[4,8,2,2048]{3,2,1,0:T(2,128)(2,1)} %copy.123), calls=%async_computation.2 | async-start | bytes 524288 | tf_op jit(solution)/shard_map/all_to_all | solution.py:121
  111.8 24.2 %copy-start.2 = (bf16[16,128,2,128]{3,2,1,0:T(2,128)(2,1)S(1)}, bf16[16,128,2,128]{3,2,1,0:T(2,128)(2,1)}, u32[]{:S(2)}) copy-start(bf16[16,128,2,128]{3,2,1,0:T(2,128)(2,1)} %reshape.167) | copy-start | bytes 3145732
  117.4 13.0 %all-to-all-start.3 = ((bf16[4,8,2,2048]{3,2,1,0:T(2,128)(2,1)}), bf16[4,8,2,2048]{3,2,1,0:T(2,128)(2,1)S(1)}, u32[]{:S(2)}, u32[]{:S(2)}) async-start(bf16[4,8,2,2048]{3,2,1,0:T(2,128)(2,1)} %fusion.10), calls=%async_computation.4 | async-start | bytes 524288 | tf_op jit(solution)/shard_map/all_to_all | solution.py:133
  121.2 60.1 %reduce-scatter.5.cloned.1.call-start = ((), (), s32[]{:S(2)}) async-start(), calls=%async_computation.8 | async-start | bytes 1310720 | tf_op jit(solution)/shard_map/reduce_scatter | solution.py:191
  136.5 64.7 %copy-start.1 = (bf16[8,2048,64]{1,2,0:T(8,128)(2,1)S(1)}, bf16[8,2048,64]{1,2,0:T(8,128)(2,1)}, u32[]{:S(2)}) copy-start(bf16[8,2048,64]{1,2,0:T(8,128)(2,1)} %param.16) | copy-start | bytes 6291460
Sparse Core Ops, SparseCore 0:
  71.1 36.8 reduce-scatter.2
  158.7 22.6 reduce-scatter.4
where the time goes:
time: 209 us; the launch traced here: 208 us
  local copies, waits for them, and re-layouts  52 us (25%)
  waiting for transfers between devices  47.8 us (23%)
  blocking collectives  44.1 us (21%)
  matrix products  26.5 us (13%)
  starting transfers between devices  18.3 us (9%)
  between operations  13.7 us (7%)
  other arithmetic  5.6 us (3%)
    reduce_scatter x1, waiting for transfers between devices, local(): lax.psum_scatter(partial_out, 'tp', scatter_dimension=2, tiled=True)  22.8 us
    all_gather x1, blocking collectives, local(): gathered_piece = lax.all_gather(attention_result, 'ep', axis=0, tiled=True)  16.3 us
    all_to_all x1, waiting for transfers between devices, local(): lax.all_to_all(normed, 'ep', split_axis=2, concat_axis=0, tiled=True)  12 us
    psum x1, blocking collectives, local(): shrunk = lax.psum(shrunk, 'tp').astype(jnp.bfloat16)  10.9 us
    unnamed x19, local copies, waits for them, and re-layouts  10.7 us
    all_to_all x1, blocking collectives, local(): lax.all_to_all(share_part, 'ep', split_axis=0, concat_axis=2, tiled=True)  10.5 us
    all_to_all x1, local copies, waits for them, and re-layouts, local(): lax.all_to_all(normed, 'ep', split_axis=2, concat_axis=0, tiled=True)  9.59 us
    all_to_all x1, waiting for transfers between devices, local(): lax.all_to_all(correction, 'ep', split_axis=0, concat_axis=0, tiled=True)  8.77 us
  transfers between devices with their start and end apart: 6, of which 4 were waited for; matrix products, arithmetic and copies ran while one was open for 26% of the time, Pallas kernels for 0%

commit v1 on v0

v1 whole, which is shorter than its diff:
```python
import functools
import math
import types

import jax
import jax.numpy as jnp
from jax import lax
from jax.experimental import pallas as pl
from jax.experimental.pallas import tpu as pltpu
from jax.sharding import PartitionSpec as P

QUERY_HEADS = 64
KEY_HEADS = 8
HEAD_SIZE = 128
EPSILON = 1e-05
THETA = 500000.0
MASKED = -1e30
MESH = pl.DeviceIdType.MESH
F32 = jnp.float32
BF16 = jnp.bfloat16
TP = 4
UNROLL_PEERS = 8


def each(count, body):
    if count <= UNROLL_PEERS:
        for i in range(1, count):
            body(i)
    else:

        @pl.loop(1, count)
        def _(i):
            body(i)


def dot(a, b):
    return jnp.dot(a, b, preferred_element_type=F32)


def body(n, names, *refs):
    s = types.SimpleNamespace(**dict(zip(names, refs)))
    e = lax.axis_index("ep")
    t = lax.axis_index("tp")
    rows, width = s.tok.shape
    requests = rows // 2
    half_rows = rows // 2
    feat = width // n
    half_feat = feat // 2
    slot_rows = s.b_recv.shape[1]
    part = s.b_recv.shape[2]
    q_cols = s.wq.shape[1]
    kv_cols = s.wkv.shape[1] // 2
    out_cols = s.wo.shape[1]
    half_out = out_cols // 2
    adapters = s.dn.shape[0]
    rank = s.dn.shape[2]
    kv_heads = kv_cols // HEAD_SIZE
    group = QUERY_HEADS // KEY_HEADS
    chunk = 512
    group_cols = group * HEAD_SIZE

    def up_peer(i):
        return lax.rem(e + i, n)

    def down_peer(i):
        return lax.rem(e + n - i, n)

    def tp_up(j):
        return lax.rem(t + j, TP)

    def tp_down(j):
        return lax.rem(t + TP - j, TP)

    def remote(src, dst, send, recv, ep=None, tp=None):
        return pltpu.make_async_remote_copy(
            src_ref=src,
            dst_ref=dst,
            send_sem=send,
            recv_sem=recv,
            device_id={"ep": e if ep is None else ep, "tp": t if tp is None else tp},
            device_id_type=MESH,
        )

    loads = {}
    for k, (name, src, dst) in enumerate(
        [
            ("tok", s.tok_hbm, s.tok),
            ("dn", s.dn_hbm, s.dn),
            ("wk", s.wk_hbm, s.wkv.at[:, :kv_cols]),
            ("wv", s.wv_hbm, s.wkv.at[:, kv_cols:]),
            ("wq", s.wq_hbm, s.wq),
            ("up", s.up_hbm, s.up),
            ("kc", s.kc_hbm, s.kc),
            ("vc", s.vc_hbm, s.vc),
            ("wo", s.wo_hbm, s.wo),
        ]
    ):
        loads[name] = pltpu.make_async_copy(src, dst, s.load_sem.at[k])
        loads[name].start()

    barrier = pltpu.get_barrier_semaphore()

    def greet(i):
        pl.semaphore_signal(
            barrier, inc=1, device_id={"ep": up_peer(i), "tp": t}, device_id_type=MESH
        )

    each(n, greet)
    for j in range(1, TP):
        pl.semaphore_signal(
            barrier, inc=1, device_id={"ep": e, "tp": tp_up(j)}, device_id_type=MESH
        )

    sub = lax.broadcasted_iota(jnp.int32, (rows, rows), 0)
    lane = lax.broadcasted_iota(jnp.int32, (rows, rows), 1)
    sub_req = jnp.right_shift(sub, 1)
    lane_req = jnp.right_shift(lane, 1)
    own_sub = jnp.zeros((rows, rows), jnp.int32)
    own_lane = jnp.zeros((rows, rows), jnp.int32)
    id_lane = jnp.zeros((rows, rows), jnp.int32)
    lane3 = lax.broadcasted_iota(jnp.int32, (rows, HEAD_SIZE), 0)
    position = jnp.zeros((rows, HEAD_SIZE), F32)
    for r in range(requests):
        value = s.idx_ref[r]
        owner = lax.div(value, jnp.int32(adapters))
        own_sub = jnp.where(sub_req == r, owner, own_sub)
        own_lane = jnp.where(lane_req == r, owner, own_lane)
        id_lane = jnp.where(lane_req == r, value - owner * adapters, id_lane)
        length = s.len_ref[r]
        s.lengths[r] = jnp.full((2 * group, HEAD_SIZE), length, jnp.int32)
        position = jnp.where(jnp.right_shift(lane3, 1) == r, length.astype(F32), position)
    position = position + (lane3 - 2 * jnp.right_shift(lane3, 1)).astype(F32)
    same = own_sub == own_lane
    before_lane = jnp.sum(
        jnp.where(same & (sub_req < lane_req), 1, 0), axis=0, keepdims=True
    )
    before_sub = jnp.sum(
        jnp.where(same & (lane_req < sub_req), 1, 0), axis=1, keepdims=True
    )
    slot_lane = own_lane[:1] * slot_rows + before_lane + (lane - 2 * lane_req)[:1]
    slot_sub = before_sub + (sub - 2 * sub_req)[:, :1]
    slots = n * slot_rows
    placing = (
        lax.broadcasted_iota(jnp.int32, (slots, rows), 0)
        == jnp.broadcast_to(slot_lane, (slots, rows))
    )
    label = jnp.sum(
        jnp.where(placing, jnp.broadcast_to(id_lane[:1], (slots, rows)), 0), axis=1, keepdims=True
    )
    label = jnp.broadcast_to(label, (slots, 128))
    for o in range(n):
        s.meta_send[o, :slot_rows] = label[o * slot_rows : (o + 1) * slot_rows]
        s.meta_send[o, slot_rows:] = jnp.broadcast_to(
            jnp.where(own_sub[:, :1] == o, slot_sub, -1), (rows, 128)
        )
    s.meta[e] = s.meta_send[e]

    loads["tok"].wait()
    for r in range(0, rows, 16):
        wide = s.tok[r : r + 16, :].astype(F32)
        factor = lax.rsqrt(jnp.mean(wide * wide, axis=-1, keepdims=True) + EPSILON)
        s.nrm[r : r + 16, :] = (wide * factor).astype(BF16)

    pl.semaphore_wait(barrier, n - 1 + TP - 1)

    def quarter(block, index):
        return (
            block,
            pl.ds(pl.multiple_of(lax.rem(index, 2) * half_rows, half_rows), half_rows),
            pl.ds(pl.multiple_of(lax.div(index, 2) * half_feat, 128), half_feat),
        )

    def a_copy(i):
        p = up_peer(i)
        src = s.nrm.at[
            pl.ds(pl.multiple_of(lax.rem(t, 2) * half_rows, half_rows), half_rows),
            pl.ds(pl.multiple_of(p * feat + lax.div(t, 2) * half_feat, 128), half_feat),
        ]
        return remote(src, s.x.at[quarter(e, t)], s.a_s.at[i], s.a_r.at[i], ep=p)

    each(n, lambda i: a_copy(i).start())

    def m_copy(i):
        p = up_peer(i)
        return remote(s.meta_send.at[p], s.meta.at[e], s.m_s.at[i], s.m_r.at[i], ep=p)

    each(n, lambda i: m_copy(i).start())

    own_part = s.nrm[:, pl.ds(pl.multiple_of(t * part, 128), part)]
    placed = dot(placing.astype(BF16), own_part).astype(BF16)
    s.b_send[...] = placed.reshape(n, slot_rows, part)

    def b_copy(i):
        p = up_peer(i)
        return remote(s.b_send.at[p], s.b_recv.at[e], s.b_s.at[i], s.b_r.at[i], ep=p)

    each(n, lambda i: b_copy(i).start())
    s.b_recv[e] = s.b_send[e]
    s.x[e] = s.nrm[:, pl.ds(pl.multiple_of(e * feat, 128), feat)]

    pair = lax.broadcasted_iota(jnp.int32, (rows, HEAD_SIZE), 1)
    upper = pair >= HEAD_SIZE // 2
    pair = jnp.where(upper, pair - HEAD_SIZE // 2, pair).astype(F32)
    angles = position * jnp.exp(pair * (-2.0 / HEAD_SIZE) * math.log(THETA))
    s.cos[...] = jnp.cos(angles)
    sine = jnp.sin(angles)
    s.sin[...] = jnp.where(upper, sine, -sine)

    def f_copy(i, j, index):
        block = down_peer(i)
        ref = s.x.at[quarter(block, index)]
        return remote(ref, ref, s.f_s.at[i, j], s.f_r.at[i, j], tp=tp_up(j))

    def forward(i):
        a_copy_in = remote(
            s.x.at[quarter(down_peer(i), t)],
            s.x.at[quarter(down_peer(i), t)],
            s.a_s.at[i],
            s.a_r.at[i],
            ep=up_peer(i),
        )
        a_copy_in.wait_recv()
        for j in range(1, TP):
            f_copy(i, j, t).start()

    each(n, forward)

    def b_in(i):
        m_copy(i).wait_recv()
        remote(
            s.b_send.at[up_peer(i)],
            s.b_recv.at[down_peer(i)],
            s.b_s.at[i],
            s.b_r.at[i],
            ep=up_peer(i),
        ).wait_recv()

    each(n, b_in)
    loads["dn"].wait()
    arrived = s.b_recv[...].reshape(slots, part)
    labels = s.meta[:, :slot_rows, :].reshape(slots, 128)
    total = jnp.zeros((slots, rank), F32)
    for a in range(adapters):
        total = total + jnp.where(labels[:, :rank] == a, dot(arrived, s.dn[a]), 0.0)
    s.sh_send[...] = jnp.concatenate([total, total], axis=1)

    def s_copy(j):
        return remote(s.sh_send, s.sh_recv.at[j], s.s_s.at[j], s.s_r.at[j], tp=tp_up(j))

    for j in range(1, TP):
        s_copy(j).start()

    def f_in(i):
        for j in range(1, TP):
            f_copy(i, j, tp_down(j)).wait_recv()

    each(n, f_in)
    loads["wk"].wait()
    loads["wv"].wait()
    row_block = s.x[...].reshape(n * rows, feat)

    def p_copy(i, c):
        p = up_peer(i)
        columns = pl.ds(c * chunk, chunk)
        return remote(
            s.p_send.at[p, :, columns],
            s.p_recv.at[i, :, columns],
            s.p_s.at[i, c],
            s.p_r.at[i, c],
            ep=p,
        )

    def ship(c, value):
        columns = slice(c * chunk, (c + 1) * chunk)
        s.p_wide[:, :, columns] = value.reshape(n, rows, chunk)
        s.p_send[:, :, columns] = value.astype(BF16).reshape(n, rows, chunk)
        each(n, lambda i: p_copy(i, c).start())

    q_chunks = q_cols // chunk
    kv_chunks = 2 * kv_cols // chunk
    for c in range(kv_chunks):
        ship(q_chunks + c, dot(row_block, s.wkv[:, c * chunk : (c + 1) * chunk]))

    for j in range(1, TP):
        s_copy(j).wait_recv()
        total_j = s.sh_recv[j]
        sh = s.sh_send[...] + total_j if j == 1 else sh + total_j
    sh = sh.astype(BF16)
    lane_slot = lax.broadcasted_iota(jnp.int32, (slots, 128), 1)
    offset = jnp.where(lane_slot >= rank, 1, 0)
    spread = jnp.concatenate(
        [
            jnp.where(labels == 2 * a + offset, sh, jnp.zeros_like(sh))
            for a in range(adapters // 2)
        ],
        axis=1,
    )
    loads["up"].wait()
    codes = s.meta[:, slot_rows:, :]
    blocks = lax.broadcasted_iota(jnp.int32, (n, rows, 128), 0)
    codes = jnp.where(codes >= 0, codes + blocks * slot_rows, -1).reshape(n * rows, 128)
    returning = jnp.concatenate(
        [
            jnp.where(
                codes[:, : min(128, slots)]
                == lax.broadcasted_iota(jnp.int32, (n * rows, min(128, slots)), 1) + 128 * k,
                1.0,
                0.0,
            )
            for k in range((slots + 127) // 128)
        ],
        axis=1,
    ).astype(BF16)
    up = s.up[...].reshape(adapters * rank, q_cols)
    loads["wq"].wait()
    for c in range(q_chunks):
        columns = slice(c * chunk, (c + 1) * chunk)
        delta = dot(spread, up[:, columns]).astype(BF16)
        ship(c, dot(row_block, s.wq[:, columns]) + dot(returning, delta))

    def p_sum(c):
        columns = slice(c * chunk, (c + 1) * chunk)
        each(n, lambda i: p_copy(i, c).wait_recv())
        value = s.p_wide[e, :, columns]
        for i in range(1, n):
            value = value + s.p_recv[i, :, columns].astype(F32)
        s.tot[:, columns] = value

    def rotate(value):
        return (value * s.cos[...] + pltpu.roll(value, HEAD_SIZE // 2, 1) * s.sin[...]).astype(BF16)

    for c in range(kv_chunks):
        p_sum(q_chunks + c)
    loads["kc"].wait()
    loads["vc"].wait()
    scale = 1.0 / math.sqrt(HEAD_SIZE)
    shape = (requests, 2, group, HEAD_SIZE)
    flat = (requests, 2 * group, HEAD_SIZE)
    slots_lane = lax.broadcasted_iota(jnp.int32, flat, 2)
    second = lax.broadcasted_iota(jnp.int32, (requests, 2, group, 1), 1) == 1

    def g_copy(i, g):
        columns = pl.ds(g * group_cols, group_cols)
        ref = s.att.at[e, :, columns]
        return remote(ref, ref, s.g_s.at[i, g], s.g_r.at[i, g], ep=up_peer(i))

    def attend(g):
        for c in range(g * group_cols // chunk, (g + 1) * group_cols // chunk):
            p_sum(c)
        base = q_cols + g * HEAD_SIZE
        key = rotate(s.tot[:, base : base + HEAD_SIZE]).astype(F32)
        value = s.tot[:, base + kv_cols : base + kv_cols + HEAD_SIZE].astype(BF16).astype(F32)
        for h in range(group):
            at = g * group_cols + h * HEAD_SIZE
            s.q3[:, h, :] = rotate(s.tot[:, at : at + HEAD_SIZE]).astype(F32)
            s.k3[:, h, :] = key
            s.v3[:, h, :] = value
        q = s.q3[...].reshape(shape)
        k = s.k3[...].reshape(shape)
        v = s.v3[...].reshape(shape)
        head = slice(g * HEAD_SIZE, (g + 1) * HEAD_SIZE)
        cached = lax.dot_general(
            q.reshape(flat).astype(BF16),
            s.kc[:, :, head],
            (((2,), (2,)), ((0,), (0,))),
            preferred_element_type=F32,
        )
        live = slots_lane < s.lengths[...]
        cached = jnp.where(live, cached * scale, MASKED)
        fresh0 = jnp.sum(q * k[:, 0:1], axis=-1, keepdims=True) * scale
        fresh1 = jnp.sum(q * k[:, 1:2], axis=-1, keepdims=True) * scale
        fresh1 = jnp.where(second, fresh1, MASKED)
        fresh0 = fresh0.reshape(requests, 2 * group, 1)
        fresh1 = fresh1.reshape(requests, 2 * group, 1)
        top = jnp.maximum(
            jnp.max(cached, axis=-1, keepdims=True), jnp.maximum(fresh0, fresh1)
        )
        cached = jnp.where(live, jnp.exp(cached - top), 0.0)
        fresh0 = jnp.exp(fresh0 - top)
        fresh1 = jnp.where(second.reshape(requests, 2 * group, 1), jnp.exp(fresh1 - top), 0.0)
        totals = jnp.sum(cached, axis=-1, keepdims=True) + (fresh0 + fresh1)
        mixture = lax.dot_general(
            (cached / totals).astype(BF16),
            s.vc[:, :, head],
            (((2,), (1,)), ((0,), (0,))),
            preferred_element_type=F32,
        ).reshape(shape)
        weight0 = (fresh0 / totals).astype(BF16).astype(F32).reshape(requests, 2, group, 1)
        weight1 = (fresh1 / totals).astype(BF16).astype(F32).reshape(requests, 2, group, 1)
        mixture = mixture + (weight0 * v[:, 0:1] + weight1 * v[:, 1:2])
        s.q3[...] = mixture.reshape(rows, group, HEAD_SIZE)
        for h in range(group):
            at = g * group_cols + h * HEAD_SIZE
            s.att[e, :, at : at + HEAD_SIZE] = s.q3[:, h, :].astype(BF16)
        each(n, lambda i: g_copy(i, g).start())

    for g in range(kv_heads):
        attend(g)

    b0 = lax.rem(t, 2)
    b1 = lax.div(t, 2)
    near = t + 1 - 2 * b0
    far = t + 2 - 4 * b1
    loads["wo"].wait()
    piece = min(chunk, half_out)
    pieces = half_out // piece

    def out_part(g, side, c):
        values = s.att[:, :, g * group_cols : (g + 1) * group_cols].reshape(n * rows, group_cols)
        columns = pl.ds(pl.multiple_of(side * half_out + c * piece, 128), piece)
        return dot(values, s.wo[g * group_cols : (g + 1) * group_cols, columns])

    def one_copy(c):
        columns = pl.ds(c * piece, piece)
        return remote(
            s.one_send.at[:, columns], s.one_recv.at[:, columns], s.o_s.at[c], s.o_r.at[c], tp=near
        )

    for g in range(kv_heads):
        each(n, lambda i: g_copy(i, g).wait_recv())
        for k, side in enumerate((1 - b0, b0)):
            for c in range(pieces):
                columns = slice(c * piece, (c + 1) * piece)
                value = out_part(g, side, c)
                if g > 0:
                    value = s.acc[k, :, columns] + value
                if k == 0 and g == kv_heads - 1:
                    s.one_send[:, columns] = value.astype(BF16)
                    one_copy(c).start()
                else:
                    s.acc[k, :, columns] = value

    def two_copy(c):
        columns = pl.ds(c * piece, piece)
        return remote(
            s.two_send.at[1 - b1, :, :, columns],
            s.two_recv.at[:, :, columns],
            s.t_s.at[c],
            s.t_r.at[c],
            tp=far,
        )

    for c in range(pieces):
        columns = slice(c * piece, (c + 1) * piece)
        one_copy(c).wait_recv()
        value = s.acc[1, :, columns] + s.one_recv[:, columns].astype(F32)
        value = value.reshape(n, rows, piece)
        for k in range(2):
            block = value[:, k * half_rows : (k + 1) * half_rows]
            s.two_wide[k, :, :, columns] = block
            s.two_send[k, :, :, columns] = block.astype(BF16)
        two_copy(c).start()

    def place(block, index, c):
        return (
            pl.ds(pl.multiple_of(lax.div(index, 2) * half_rows, half_rows), half_rows),
            pl.ds(
                pl.multiple_of(block * out_cols + lax.rem(index, 2) * half_out + c * piece, 128),
                piece,
            ),
        )

    def three_copy(i, c):
        p = up_peer(i)
        return remote(
            s.three_send.at[p, :, pl.ds(c * piece, piece)],
            s.out.at[place(e, t, c)],
            s.h_s.at[i, c],
            s.h_r.at[i, c],
            ep=p,
        )

    def four_copy(i, j, c, block, index):
        ref = s.out.at[place(block, index, c)]
        return remote(ref, ref, s.r_s.at[i, j, c], s.r_r.at[i, j, c], tp=tp_up(j))

    for c in range(pieces):
        columns = slice(c * piece, (c + 1) * piece)
        two_copy(c).wait_recv()
        value = s.two_wide[b1, :, :, columns] + s.two_recv[:, :, columns].astype(F32)
        s.three_send[:, :, columns] = value.astype(BF16)
        each(n, lambda i: three_copy(i, c).start())
        s.out[place(e, t, c)] = s.three_send[e, :, columns]
        for j in range(1, TP):
            four_copy(0, j, c, e, t).start()

    for c in range(pieces):

        def pass_on(i):
            ref = s.out.at[place(down_peer(i), t, c)]
            remote(ref, ref, s.h_s.at[i, c], s.h_r.at[i, c], ep=up_peer(i)).wait_recv()
            for j in range(1, TP):
                four_copy(i, j, c, down_peer(i), t).start()

        each(n, pass_on)

    def last(i):
        for c in range(pieces):
            for j in range(1, TP):
                four_copy(i, j, c, down_peer(i), tp_down(j)).wait_recv()

    last(0)
    each(n, last)
    final = pltpu.make_async_copy(s.out, s.out_hbm, s.load_sem.at[0])
    final.start()

    def drain(i):
        a_copy(i).wait_send()
        m_copy(i).wait_send()
        b_copy(i).wait_send()
        for c in range(q_chunks + kv_chunks):
            p_copy(i, c).wait_send()
        for g in range(kv_heads):
            g_copy(i, g).wait_send()
        for c in range(pieces):
            three_copy(i, c).wait_send()
            for j in range(1, TP):
                four_copy(i, j, c, down_peer(i), t).wait_send()
        for j in range(1, TP):
            f_copy(i, j, t).wait_send()

    each(n, drain)
    for j in range(1, TP):
        s_copy(j).wait_send()
        for c in range(pieces):
            four_copy(0, j, c, e, t).wait_send()
    for c in range(pieces):
        one_copy(c).wait_send()
        two_copy(c).wait_send()
    final.wait()


def local(
    tokens,
    query_weight,
    key_weight,
    value_weight,
    output_weight,
    adapter_down_maps,
    adapter_up_maps,
    rotated_cache_keys,
    cached_value_rows,
    adapter_index,
    cached_lengths,
):
    n = lax.axis_size("ep")
    requests, steps, width = tokens.shape
    rows = requests * steps
    feat, q_cols = query_weight.shape
    kv_cols = key_weight.shape[1]
    all_cols = q_cols + 2 * kv_cols
    out_cols = output_weight.shape[1]
    half_out = out_cols // 2
    part = adapter_down_maps.shape[1]
    capacity = max(2, (2 * requests + n - 1) // n)
    slot_rows = max(16, -(-capacity * steps // 16) * 16)
    slots = n * slot_rows
    group = QUERY_HEADS // KEY_HEADS
    kv_heads = kv_cols // HEAD_SIZE
    chunks = all_cols // 512
    pieces = half_out // min(512, half_out)
    vmem = pltpu.VMEM
    dma = pltpu.SemaphoreType.DMA
    scratch = dict(
        tok=vmem((rows, width), BF16),
        nrm=vmem((rows, width), BF16),
        wq=vmem(query_weight.shape, BF16),
        wkv=vmem((feat, 2 * kv_cols), BF16),
        wo=vmem(output_weight.shape, BF16),
        dn=vmem(adapter_down_maps.shape, BF16),
        up=vmem(adapter_up_maps.shape, BF16),
        kc=vmem(rotated_cache_keys.shape, BF16),
        vc=vmem(cached_value_rows.shape, BF16),
        x=vmem((n, rows, feat), BF16),
        b_send=vmem((n, slot_rows, part), BF16),
        b_recv=vmem((n, slot_rows, part), BF16),
        meta_send=vmem((n, slot_rows + rows, 128), jnp.int32),
        meta=vmem((n, slot_rows + rows, 128), jnp.int32),
        sh_send=vmem((slots, 128), F32),
        sh_recv=vmem((TP, slots, 128), F32),
        p_wide=vmem((n, rows, all_cols), F32),
        p_send=vmem((n, rows, all_cols), BF16),
        p_recv=vmem((n, rows, all_cols), BF16),
        tot=vmem((rows, all_cols), F32),
        cos=vmem((rows, HEAD_SIZE), F32),
        sin=vmem((rows, HEAD_SIZE), F32),
        lengths=vmem((requests, 2 * group, HEAD_SIZE), jnp.int32),
        q3=vmem((rows, group, HEAD_SIZE), F32),
        k3=vmem((rows, group, HEAD_SIZE), F32),
        v3=vmem((rows, group, HEAD_SIZE), F32),
        att=vmem((n, rows, q_cols), BF16),
        acc=vmem((2, n * rows, half_out), F32),
        one_send=vmem((n * rows, half_out), BF16),
        one_recv=vmem((n * rows, half_out), BF16),
        two_wide=vmem((2, n, rows // 2, half_out), F32),
        two_send=vmem((2, n, rows // 2, half_out), BF16),
        two_recv=vmem((n, rows // 2, half_out), BF16),
        three_send=vmem((n, rows // 2, half_out), BF16),
        out=vmem((rows, width), BF16),
        load_sem=dma((9,)),
        a_s=dma((n,)),
        a_r=dma((n,)),
        m_s=dma((n,)),
        m_r=dma((n,)),
        b_s=dma((n,)),
        b_r=dma((n,)),
        f_s=dma((n, TP)),
        f_r=dma((n, TP)),
        s_s=dma((TP,)),
        s_r=dma((TP,)),
        p_s=dma((n, chunks)),
        p_r=dma((n, chunks)),
        g_s=dma((n, kv_heads)),
        g_r=dma((n, kv_heads)),
        o_s=dma((pieces,)),
        o_r=dma((pieces,)),
        t_s=dma((pieces,)),
        t_r=dma((pieces,)),
        h_s=dma((n, pieces)),
        h_r=dma((n, pieces)),
        r_s=dma((n, TP, pieces)),
        r_r=dma((n, TP, pieces)),
    )
    operands = [
        "idx_ref",
        "len_ref",
        "tok_hbm",
        "wq_hbm",
        "wk_hbm",
        "wv_hbm",
        "wo_hbm",
        "dn_hbm",
        "up_hbm",
        "kc_hbm",
        "vc_hbm",
        "out_hbm",
    ]
    out = pl.pallas_call(
        functools.partial(body, n, operands + list(scratch)),
        out_shape=jax.ShapeDtypeStruct((rows, width), BF16),
        in_specs=[pl.BlockSpec(memory_space=pltpu.SMEM)] * 2
        + [pl.BlockSpec(memory_space=pl.ANY)] * 9,
        out_specs=pl.BlockSpec(memory_space=pl.ANY),
        scratch_shapes=list(scratch.values()),
        compiler_params=pltpu.CompilerParams(
            collective_id=0, has_side_effects=True, vmem_limit_bytes=60 * 2**20
        ),
        name="sublayer",
    )(
        adapter_index,
        cached_lengths,
        tokens.reshape(rows, width),
        query_weight,
        key_weight,
        value_weight,
        output_weight,
        adapter_down_maps,
        adapter_up_maps,
        rotated_cache_keys,
        cached_value_rows,
    )
    return out.reshape(tokens.shape)


def solution(mesh):
    return jax.shard_map(
        local,
        mesh=mesh,
        in_specs=(
            P(("groups", "ep"), None, None),
            P("ep", "tp"),
            P("ep", "tp"),
            P("ep", "tp"),
            P("tp", "ep"),
            P("ep", "tp", None),
            P("ep", None, "tp"),
            P(("groups", "ep"), None, "tp"),
            P(("groups", "ep"), None, "tp"),
            P(("groups", "ep")),
            P(("groups", "ep")),
        ),
        out_specs=P(("groups", "ep"), None, None),
        check_vma=False,
    )
```

time: 209 us -> 73 us (0.35)
  Pallas kernels: 0 us -> 63.8 us
  waiting for transfers between devices: 47.8 us -> 0 us
  blocking collectives: 44.1 us -> 0 us
  local copies, waits for them, and re-layouts: 52 us -> 8.98 us
  matrix products: 26.5 us -> 0 us
  starting transfers between devices: 18.3 us -> 0 us
  between operations: 13.7 us -> 0.01 us
  other arithmetic: 5.6 us -> 0 us
    pallas_call x0 -> x1, Pallas kernels: none -> 63.8 us  [local(): pl.pallas_call(functools.partial(body, n, operands + list(scratch)), out_...]
    dot_general x13 -> x0, matrix products: 26.5 us -> none  [the longest x1 5.77 us: local(): jnp.einsum('ocsd,ocdr->ocsr', arrived_rows, selected_down, preferred_elem...]
    all_to_all x4 -> x0, waiting for transfers between devices: 24.9 us -> none  [the longest x1 12 us: local(): lax.all_to_all(normed, 'ep', split_axis=2, concat_axis=0, tiled=True)]
    all_gather x2 -> x0, blocking collectives: 22.8 us -> none  [the longest x1 16.3 us: local(): gathered_piece = lax.all_gather(attention_result, 'ep', axis=0, tiled=True)]
    reduce_scatter x2 -> x0, waiting for transfers between devices: 22.8 us -> none  [the longest x1 22.8 us: local(): lax.psum_scatter(partial_out, 'tp', scatter_dimension=2, tiled=True)]
    all_to_all x4 -> x0, starting transfers between devices: 18.3 us -> none  [the longest x1 6.32 us: local(): lax.all_to_all(normed, 'ep', split_axis=2, concat_axis=0, tiled=True)]
    gather x2 -> x0, local copies, waits for them, and re-layouts: 11.3 us -> none  [the longest x1 6.47 us: local(): selected_up = jnp.take(adapter_up_maps, selected_rows, axis=0)]
    psum x1 -> x0, blocking collectives: 10.9 us -> none  [local(): shrunk = lax.psum(shrunk, 'tp').astype(jnp.bfloat16)]
  transfers between devices with their start and end apart: 6 -> 0, of which waited for: 4 -> 0; matrix products, arithmetic and copies ran while one was open for 26% -> 0% of each run, Pallas kernels for 0% -> 0%
where the time goes in v1:
time: 73 us; the launch traced here: 72.7 us
  Pallas kernels  63.8 us (87%)
  local copies, waits for them, and re-layouts  8.98 us (12%)
    pallas_call x1, Pallas kernels, local(): pl.pallas_call(functools.partial(body, n, operands + list(scratch)), out_...  63.8 us
    unnamed x1, local copies, waits for them, and re-layouts  4.78 us
    reshape x1, local copies, waits for them, and re-layouts, local(): return out.reshape(tokens.shape)  2.17 us
    reshape x1, local copies, waits for them, and re-layouts, local(): tokens.reshape(rows, width)  2.03 us

profile of v1, /device:TPU:0, one launch (start us, length us, event | category | flops | bytes accessed | tf_op | source)
XLA Modules:
  0.0 72.7 jit_solution(10257843571365054385)
XLA Ops:
  0.0 2.0 %reshape.6.refs_2_ = bf16[32,8192]{1,0:T(8,128)(2,1)} reshape(bf16[16,2,8192]{2,1,0:T(2,128)(2,1)} %param.11) | data formatting | bytes 1048576 | tf_op jit(solution)/shard_map/reshape | solution.py:652
  2.0 4.8 %copy.12.refs_7_ = bf16[8,2048,64]{2,1,0:T(8,128)(2,1)} copy(bf16[8,2048,64]{1,2,0:T(8,128)(2,1)} %param.16) | data formatting | bytes 4194304 | tf_op args[5]
  6.8 63.8 %sublayer.1 = bf16[32,8192]{1,0:T(8,128)(2,1)} custom-call(s32[16]{0:T(128)} %refs_0_.1, s32[16]{0:T(128)} %refs_1_.1, bf16[32,8192]{1,0:T(8,128)(2,1)} %reshape.6.refs_2_, bf16[2048,2048]{1,0:T(8,128)(2,1)} %refs_3_.1, bf16[2048,256]{1,0:T(8,128)(2,1)} %refs_4_.1, bf16[2048,256]{1,0:T(8,128)(2,1)} %refs_5_.1, bf16[2048,2048]{1,0:T(8,128)(2,1)} %refs_6_.1, ...), custom_call_target="tpu_custom_call" | custom-call | tf_op jit(solution)/shard_map/sublayer/pallas_call | solution.py:638
  70.6 2.2 %reshape.7 = bf16[16,2,8192]{2,1,0:T(2,128)(2,1)} reshape(bf16[32,8192]{1,0:T(8,128)(2,1)} %sublayer.1) | data formatting | bytes 1048576 | tf_op jit(solution)/shard_map/reshape | solution.py:662

commit v2 on v1

--- a/solution.py
+++ b/solution.py
@@ -53,7 +53,7 @@
     out_cols = s.wo.shape[1]
     half_out = out_cols // 2
     adapters = s.dn.shape[0]
-    rank = s.dn.shape[2]
+    rank = s.dn.shape[1]
     kv_heads = kv_cols // HEAD_SIZE
     group = QUERY_HEADS // KEY_HEADS
     chunk = 512
@@ -111,49 +111,41 @@
             barrier, inc=1, device_id={"ep": e, "tp": tp_up(j)}, device_id_type=MESH
         )
 
-    sub = lax.broadcasted_iota(jnp.int32, (rows, rows), 0)
-    lane = lax.broadcasted_iota(jnp.int32, (rows, rows), 1)
+    square = (1, rows, rows)
+    sub = lax.broadcasted_iota(jnp.int32, square, 1)
+    lane = lax.broadcasted_iota(jnp.int32, square, 2)
     sub_req = jnp.right_shift(sub, 1)
     lane_req = jnp.right_shift(lane, 1)
-    own_sub = jnp.zeros((rows, rows), jnp.int32)
-    own_lane = jnp.zeros((rows, rows), jnp.int32)
-    id_lane = jnp.zeros((rows, rows), jnp.int32)
+    slots = n * slot_rows
+
+    def slots_of(flags):
+        flags_sub = jnp.sum(jnp.where(sub == lane, flags, 0), axis=2, keepdims=True)
+        before_lane = jnp.sum(jnp.where(sub_req < lane_req, flags_sub, 0), axis=1, keepdims=True)
+        before_sub = jnp.sum(jnp.where(lane_req < sub_req, flags, 0), axis=2, keepdims=True)
+        return (
+            flags_sub,
+            before_lane + (lane - 2 * lane_req)[:, :1],
+            before_sub + (sub - 2 * sub_req)[:, :, :1],
+        )
+
+    tile_req = jnp.right_shift(lax.broadcasted_iota(jnp.int32, (8, 128), 1), 1)
     lane3 = lax.broadcasted_iota(jnp.int32, (rows, HEAD_SIZE), 0)
     position = jnp.zeros((rows, HEAD_SIZE), F32)
+    own_ids = jnp.zeros((8, 128), jnp.int32)
     for r in range(requests):
-        value = s.idx_ref[r]
-        owner = lax.div(value, jnp.int32(adapters))
-        own_sub = jnp.where(sub_req == r, owner, own_sub)
-        own_lane = jnp.where(lane_req == r, owner, own_lane)
-        id_lane = jnp.where(lane_req == r, value - owner * adapters, id_lane)
+        own_ids = jnp.where(tile_req == r, s.idx_ref[r], own_ids)
         length = s.len_ref[r]
         s.lengths[r] = jnp.full((2 * group, HEAD_SIZE), length, jnp.int32)
         position = jnp.where(jnp.right_shift(lane3, 1) == r, length.astype(F32), position)
     position = position + (lane3 - 2 * jnp.right_shift(lane3, 1)).astype(F32)
-    same = own_sub == own_lane
-    before_lane = jnp.sum(
-        jnp.where(same & (sub_req < lane_req), 1, 0), axis=0, keepdims=True
-    )
-    before_sub = jnp.sum(
-        jnp.where(same & (lane_req < sub_req), 1, 0), axis=1, keepdims=True
-    )
-    slot_lane = own_lane[:1] * slot_rows + before_lane + (lane - 2 * lane_req)[:1]
-    slot_sub = before_sub + (sub - 2 * sub_req)[:, :1]
-    slots = n * slot_rows
-    placing = (
-        lax.broadcasted_iota(jnp.int32, (slots, rows), 0)
-        == jnp.broadcast_to(slot_lane, (slots, rows))
-    )
-    label = jnp.sum(
-        jnp.where(placing, jnp.broadcast_to(id_lane[:1], (slots, rows)), 0), axis=1, keepdims=True
-    )
-    label = jnp.broadcast_to(label, (slots, 128))
-    for o in range(n):
-        s.meta_send[o, :slot_rows] = label[o * slot_rows : (o + 1) * slot_rows]
-        s.meta_send[o, slot_rows:] = jnp.broadcast_to(
-            jnp.where(own_sub[:, :1] == o, slot_sub, -1), (rows, 128)
-        )
-    s.meta[e] = s.meta_send[e]
+    s.id_send[...] = own_ids
+    s.ids[e] = own_ids
+    owners = lax.broadcasted_iota(jnp.int32, (n, 1, rows), 0)
+    own_row = own_ids[:1, :rows].reshape(1, 1, rows) - owners * adapters
+    flags = jnp.where((own_row >= 0) & (own_row < adapters), 1, 0)
+    _, slot_lane, _ = slots_of(flags)
+    placing = (lax.broadcasted_iota(jnp.int32, (n, slot_rows, rows), 1) == slot_lane) & (flags > 0)
+    placing = jnp.where(placing, 1.0, 0.0).reshape(slots, rows)
 
     loads["tok"].wait()
     for r in range(0, rows, 16):
@@ -182,7 +174,7 @@
 
     def m_copy(i):
         p = up_peer(i)
-        return remote(s.meta_send.at[p], s.meta.at[e], s.m_s.at[i], s.m_r.at[i], ep=p)
+        return remote(s.id_send, s.ids.at[e], s.m_s.at[i], s.m_r.at[i], ep=p)
 
     each(n, lambda i: m_copy(i).start())
 
@@ -206,24 +198,28 @@
     sine = jnp.sin(angles)
     s.sin[...] = jnp.where(upper, sine, -sine)
 
-    def f_copy(i, j, index):
-        block = down_peer(i)
-        ref = s.x.at[quarter(block, index)]
-        return remote(ref, ref, s.f_s.at[i, j], s.f_r.at[i, j], tp=tp_up(j))
+    b0 = lax.rem(t, 2)
+    b1 = lax.div(t, 2)
+    near = t + 1 - 2 * b0
+    far = t + 2 - 4 * b1
+    across = near + 2 - 4 * b1
+
+    def f_copy(i, k, index):
+        ref = s.x.at[quarter(down_peer(i), index)]
+        return remote(ref, ref, s.f_s.at[i, k], s.f_r.at[i, k], tp=far if k == 1 else near)
 
     def forward(i):
-        a_copy_in = remote(
-            s.x.at[quarter(down_peer(i), t)],
-            s.x.at[quarter(down_peer(i), t)],
-            s.a_s.at[i],
-            s.a_r.at[i],
-            ep=up_peer(i),
-        )
-        a_copy_in.wait_recv()
-        for j in range(1, TP):
-            f_copy(i, j, t).start()
+        ref = s.x.at[quarter(down_peer(i), t)]
+        remote(ref, ref, s.a_s.at[i], s.a_r.at[i], ep=up_peer(i)).wait_recv()
+        f_copy(i, 1, t).start()
+        f_copy(i, 0, t).start()
+
+    def forward_far(i):
+        f_copy(i, 1, far).wait_recv()
+        f_copy(i, 2, far).start()
 
     each(n, forward)
+    each(n, forward_far)
 
     def b_in(i):
         m_copy(i).wait_recv()
@@ -238,11 +234,25 @@
     each(n, b_in)
     loads["dn"].wait()
     arrived = s.b_recv[...].reshape(slots, part)
-    labels = s.meta[:, :slot_rows, :].reshape(slots, 128)
-    total = jnp.zeros((slots, rank), F32)
-    for a in range(adapters):
-        total = total + jnp.where(labels[:, :rank] == a, dot(arrived, s.dn[a]), 0.0)
-    s.sh_send[...] = jnp.concatenate([total, total], axis=1)
+    ids = s.ids[:, :1, :rows] - e * adapters
+    flags = jnp.where((ids >= 0) & (ids < adapters), 1, 0)
+    flags_sub, slot_lane, slot_sub = slots_of(flags)
+    taken = (lax.broadcasted_iota(jnp.int32, (n, slot_rows, rows), 1) == slot_lane) & (flags > 0)
+    labels = jnp.sum(jnp.where(taken, ids, 0), axis=2, keepdims=True)
+    labels = jnp.broadcast_to(labels, (n, slot_rows, 128)).reshape(slots, 128)
+    lane_slot = lax.broadcasted_iota(jnp.int32, (slots, 128), 1)
+    offset = jnp.where(lane_slot >= rank, 1, 0)
+    down = lax.dot_general(
+        arrived,
+        s.dn[...].reshape(adapters * rank, part),
+        (((1,), (1,)), ((), ())),
+        preferred_element_type=F32,
+    )
+    total = jnp.zeros((slots, 128), F32)
+    for a in range(adapters // 2):
+        block = down[:, 128 * a : 128 * (a + 1)]
+        total = total + jnp.where(labels == 2 * a + offset, block, 0.0)
+    s.sh_send[...] = total + pltpu.roll(total, rank, 1)
 
     def s_copy(j):
         return remote(s.sh_send, s.sh_recv.at[j], s.s_s.at[j], s.s_r.at[j], tp=tp_up(j))
@@ -251,8 +261,8 @@
         s_copy(j).start()
 
     def f_in(i):
-        for j in range(1, TP):
-            f_copy(i, j, tp_down(j)).wait_recv()
+        f_copy(i, 0, near).wait_recv()
+        f_copy(i, 2, across).wait_recv()
 
     each(n, f_in)
     loads["wk"].wait()
@@ -286,8 +296,6 @@
         total_j = s.sh_recv[j]
         sh = s.sh_send[...] + total_j if j == 1 else sh + total_j
     sh = sh.astype(BF16)
-    lane_slot = lax.broadcasted_iota(jnp.int32, (slots, 128), 1)
-    offset = jnp.where(lane_slot >= rank, 1, 0)
     spread = jnp.concatenate(
         [
             jnp.where(labels == 2 * a + offset, sh, jnp.zeros_like(sh))
@@ -296,21 +304,10 @@
         axis=1,
     )
     loads["up"].wait()
-    codes = s.meta[:, slot_rows:, :]
-    blocks = lax.broadcasted_iota(jnp.int32, (n, rows, 128), 0)
-    codes = jnp.where(codes >= 0, codes + blocks * slot_rows, -1).reshape(n * rows, 128)
-    returning = jnp.concatenate(
-        [
-            jnp.where(
-                codes[:, : min(128, slots)]
-                == lax.broadcasted_iota(jnp.int32, (n * rows, min(128, slots)), 1) + 128 * k,
-                1.0,
-                0.0,
-            )
-            for k in range((slots + 127) // 128)
-        ],
-        axis=1,
-    ).astype(BF16)
+    block = lax.broadcasted_iota(jnp.int32, (n, rows, 1), 0) * slot_rows
+    codes = jnp.where(flags_sub > 0, slot_sub + block, -1)
+    returning = lax.broadcasted_iota(jnp.int32, (n, rows, slots), 2) == codes
+    returning = jnp.where(returning, 1.0, 0.0).reshape(n * rows, slots).astype(BF16)
     up = s.up[...].reshape(adapters * rank, q_cols)
     loads["wq"].wait()
     for c in range(q_chunks):
@@ -397,10 +394,6 @@
     for g in range(kv_heads):
         attend(g)
 
-    b0 = lax.rem(t, 2)
-    b1 = lax.div(t, 2)
-    near = t + 1 - 2 * b0
-    far = t + 2 - 4 * b1
     loads["wo"].wait()
     piece = min(chunk, half_out)
     pieces = half_out // piece
@@ -470,9 +463,15 @@
             ep=p,
         )
 
-    def four_copy(i, j, c, block, index):
-        ref = s.out.at[place(block, index, c)]
-        return remote(ref, ref, s.r_s.at[i, j, c], s.r_r.at[i, j, c], tp=tp_up(j))
+    def four_copy(i, k, c, index):
+        ref = s.out.at[place(down_peer(i), index, c)]
+        return remote(
+            ref, ref, s.r_s.at[i, k, c], s.r_r.at[i, k, c], tp=far if k == 1 else near
+        )
+
+    def pass_far(i, c):
+        four_copy(i, 1, c, far).wait_recv()
+        four_copy(i, 2, c, far).start()
 
     for c in range(pieces):
         columns = slice(c * piece, (c + 1) * piece)
@@ -481,23 +480,25 @@
         s.three_send[:, :, columns] = value.astype(BF16)
         each(n, lambda i: three_copy(i, c).start())
         s.out[place(e, t, c)] = s.three_send[e, :, columns]
-        for j in range(1, TP):
-            four_copy(0, j, c, e, t).start()
+        four_copy(0, 1, c, t).start()
+        four_copy(0, 0, c, t).start()
 
     for c in range(pieces):
 
         def pass_on(i):
             ref = s.out.at[place(down_peer(i), t, c)]
             remote(ref, ref, s.h_s.at[i, c], s.h_r.at[i, c], ep=up_peer(i)).wait_recv()
-            for j in range(1, TP):
-                four_copy(i, j, c, down_peer(i), t).start()
-
+            four_copy(i, 1, c, t).start()
+            four_copy(i, 0, c, t).start()
+
+        pass_far(0, c)
         each(n, pass_on)
+        each(n, lambda i: pass_far(i, c))
 
     def last(i):
         for c in range(pieces):
-            for j in range(1, TP):
-                four_copy(i, j, c, down_peer(i), tp_down(j)).wait_recv()
+            four_copy(i, 0, c, near).wait_recv()
+            four_copy(i, 2, c, across).wait_recv()
 
     last(0)
     each(n, last)
@@ -514,17 +515,17 @@
             g_copy(i, g).wait_send()
         for c in range(pieces):
             three_copy(i, c).wait_send()
-            for j in range(1, TP):
-                four_copy(i, j, c, down_peer(i), t).wait_send()
-        for j in range(1, TP):
-            f_copy(i, j, t).wait_send()
+            for k in range(3):
+                four_copy(i, k, c, t).wait_send()
+        for k in range(3):
+            f_copy(i, k, t).wait_send()
 
     each(n, drain)
     for j in range(1, TP):
         s_copy(j).wait_send()
-        for c in range(pieces):
-            four_copy(0, j, c, e, t).wait_send()
     for c in range(pieces):
+        for k in range(3):
+            four_copy(0, k, c, t).wait_send()
         one_copy(c).wait_send()
         two_copy(c).wait_send()
     final.wait()
@@ -551,7 +552,7 @@
     all_cols = q_cols + 2 * kv_cols
     out_cols = output_weight.shape[1]
     half_out = out_cols // 2
-    part = adapter_down_maps.shape[1]
+    adapters, part, rank = adapter_down_maps.shape
     capacity = max(2, (2 * requests + n - 1) // n)
     slot_rows = max(16, -(-capacity * steps // 16) * 16)
     slots = n * slot_rows
@@ -567,15 +568,15 @@
         wq=vmem(query_weight.shape, BF16),
         wkv=vmem((feat, 2 * kv_cols), BF16),
         wo=vmem(output_weight.shape, BF16),
-        dn=vmem(adapter_down_maps.shape, BF16),
+        dn=vmem((adapters, rank, part), BF16),
         up=vmem(adapter_up_maps.shape, BF16),
         kc=vmem(rotated_cache_keys.shape, BF16),
         vc=vmem(cached_value_rows.shape, BF16),
         x=vmem((n, rows, feat), BF16),
         b_send=vmem((n, slot_rows, part), BF16),
         b_recv=vmem((n, slot_rows, part), BF16),
-        meta_send=vmem((n, slot_rows + rows, 128), jnp.int32),
-        meta=vmem((n, slot_rows + rows, 128), jnp.int32),
+        id_send=vmem((8, 128), jnp.int32),
+        ids=vmem((n, 8, 128), jnp.int32),
         sh_send=vmem((slots, 128), F32),
         sh_recv=vmem((TP, slots, 128), F32),
         p_wide=vmem((n, rows, all_cols), F32),
@@ -654,7 +655,7 @@
         key_weight,
         value_weight,
         output_weight,
-        adapter_down_maps,
+        jnp.swapaxes(adapter_down_maps, 1, 2),
         adapter_up_maps,
         rotated_cache_keys,
         cached_value_rows,

time: 73 us -> 69.3 us (0.949)
  local copies, waits for them, and re-layouts: 8.98 us -> 4.2 us
    unnamed x1 -> x0, local copies, waits for them, and re-layouts: 4.78 us -> none
where the time goes in v2:
time: 69.3 us; the launch traced here: 68.4 us
  Pallas kernels  64.2 us (93%)
  local copies, waits for them, and re-layouts  4.2 us (6%)
    pallas_call x1, Pallas kernels, local(): pl.pallas_call(functools.partial(body, n, operands + list(scratch)), out_...  64.2 us
    reshape x1, local copies, waits for them, and re-layouts, local(): return out.reshape(tokens.shape)  2.17 us
    reshape x1, local copies, waits for them, and re-layouts, local(): tokens.reshape(rows, width)  2.03 us

profile of v2, /device:TPU:0, one launch (start us, length us, event | category | flops | bytes accessed | tf_op | source)
XLA Modules:
  0.0 68.4 jit_solution(17136026067593498793)
XLA Ops:
  0.0 2.0 %reshape.6.refs_2_ = bf16[32,8192]{1,0:T(8,128)(2,1)} reshape(bf16[16,2,8192]{2,1,0:T(2,128)(2,1)} %param.11) | data formatting | bytes 1048576 | tf_op jit(solution)/shard_map/reshape | solution.py:653
  2.0 64.2 %sublayer.1 = bf16[32,8192]{1,0:T(8,128)(2,1)} custom-call(s32[16]{0:T(128)} %refs_0_.1, s32[16]{0:T(128)} %refs_1_.1, bf16[32,8192]{1,0:T(8,128)(2,1)} %reshape.6.refs_2_, bf16[2048,2048]{1,0:T(8,128)(2,1)} %refs_3_.1, bf16[2048,256]{1,0:T(8,128)(2,1)} %refs_4_.1, bf16[2048,256]{1,0:T(8,128)(2,1)} %refs_5_.1, bf16[2048,2048]{1,0:T(8,128)(2,1)} %refs_6_.1, ...), custom_call_target="tpu_custom_call" | custom-call | tf_op jit(solution)/shard_map/sublayer/pallas_call | solution.py:639
  66.2 2.2 %reshape.7 = bf16[16,2,8192]{2,1,0:T(2,128)(2,1)} reshape(bf16[32,8192]{1,0:T(8,128)(2,1)} %sublayer.1) | data formatting | bytes 1048576 | tf_op jit(solution)/shard_map/reshape | solution.py:663

commit v3 on v2

--- a/solution.py
+++ b/solution.py
@@ -59,11 +59,13 @@
     chunk = 512
     group_cols = group * HEAD_SIZE
 
-    def up_peer(i):
-        return lax.rem(e + i, n)
-
-    def down_peer(i):
-        return lax.rem(e + n - i, n)
+    def partner(i):
+        both = 0
+        bit = 1
+        while bit < n:
+            both = both + bit * (lax.rem(lax.div(e, bit), 2) * ((i // bit) % 2))
+            bit *= 2
+        return e + i - 2 * both
 
     def tp_up(j):
         return lax.rem(t + j, TP)
@@ -102,7 +104,7 @@
 
     def greet(i):
         pl.semaphore_signal(
-            barrier, inc=1, device_id={"ep": up_peer(i), "tp": t}, device_id_type=MESH
+            barrier, inc=1, device_id={"ep": partner(i), "tp": t}, device_id_type=MESH
         )
 
     each(n, greet)
@@ -163,7 +165,7 @@
         )
 
     def a_copy(i):
-        p = up_peer(i)
+        p = partner(i)
         src = s.nrm.at[
             pl.ds(pl.multiple_of(lax.rem(t, 2) * half_rows, half_rows), half_rows),
             pl.ds(pl.multiple_of(p * feat + lax.div(t, 2) * half_feat, 128), half_feat),
@@ -173,7 +175,7 @@
     each(n, lambda i: a_copy(i).start())
 
     def m_copy(i):
-        p = up_peer(i)
+        p = partner(i)
         return remote(s.id_send, s.ids.at[e], s.m_s.at[i], s.m_r.at[i], ep=p)
 
     each(n, lambda i: m_copy(i).start())
@@ -183,7 +185,7 @@
     s.b_send[...] = placed.reshape(n, slot_rows, part)
 
     def b_copy(i):
-        p = up_peer(i)
+        p = partner(i)
         return remote(s.b_send.at[p], s.b_recv.at[e], s.b_s.at[i], s.b_r.at[i], ep=p)
 
     each(n, lambda i: b_copy(i).start())
@@ -205,12 +207,12 @@
     across = near + 2 - 4 * b1
 
     def f_copy(i, k, index):
-        ref = s.x.at[quarter(down_peer(i), index)]
+        ref = s.x.at[quarter(partner(i), index)]
         return remote(ref, ref, s.f_s.at[i, k], s.f_r.at[i, k], tp=far if k == 1 else near)
 
     def forward(i):
-        ref = s.x.at[quarter(down_peer(i), t)]
-        remote(ref, ref, s.a_s.at[i], s.a_r.at[i], ep=up_peer(i)).wait_recv()
+        ref = s.x.at[quarter(partner(i), t)]
+        remote(ref, ref, s.a_s.at[i], s.a_r.at[i], ep=partner(i)).wait_recv()
         f_copy(i, 1, t).start()
         f_copy(i, 0, t).start()
 
@@ -224,11 +226,11 @@
     def b_in(i):
         m_copy(i).wait_recv()
         remote(
-            s.b_send.at[up_peer(i)],
-            s.b_recv.at[down_peer(i)],
+            s.b_send.at[partner(i)],
+            s.b_recv.at[partner(i)],
             s.b_s.at[i],
             s.b_r.at[i],
-            ep=up_peer(i),
+            ep=partner(i),
         ).wait_recv()
 
     each(n, b_in)
@@ -270,7 +272,7 @@
     row_block = s.x[...].reshape(n * rows, feat)
 
     def p_copy(i, c):
-        p = up_peer(i)
+        p = partner(i)
         columns = pl.ds(c * chunk, chunk)
         return remote(
             s.p_send.at[p, :, columns],
@@ -282,7 +284,7 @@
 
     def ship(c, value):
         columns = slice(c * chunk, (c + 1) * chunk)
-        s.p_wide[:, :, columns] = value.reshape(n, rows, chunk)
+        s.p_wide[:, columns] = value
         s.p_send[:, :, columns] = value.astype(BF16).reshape(n, rows, chunk)
         each(n, lambda i: p_copy(i, c).start())
 
@@ -290,6 +292,11 @@
     kv_chunks = 2 * kv_cols // chunk
     for c in range(kv_chunks):
         ship(q_chunks + c, dot(row_block, s.wkv[:, c * chunk : (c + 1) * chunk]))
+
+    loads["wq"].wait()
+    for c in range(q_chunks):
+        columns = slice(c * chunk, (c + 1) * chunk)
+        s.p_wide[:, columns] = dot(row_block, s.wq[:, columns])
 
     for j in range(1, TP):
         s_copy(j).wait_recv()
@@ -309,16 +316,15 @@
     returning = lax.broadcasted_iota(jnp.int32, (n, rows, slots), 2) == codes
     returning = jnp.where(returning, 1.0, 0.0).reshape(n * rows, slots).astype(BF16)
     up = s.up[...].reshape(adapters * rank, q_cols)
-    loads["wq"].wait()
     for c in range(q_chunks):
         columns = slice(c * chunk, (c + 1) * chunk)
         delta = dot(spread, up[:, columns]).astype(BF16)
-        ship(c, dot(row_block, s.wq[:, columns]) + dot(returning, delta))
+        ship(c, s.p_wide[:, columns] + dot(returning, delta))
 
     def p_sum(c):
         columns = slice(c * chunk, (c + 1) * chunk)
         each(n, lambda i: p_copy(i, c).wait_recv())
-        value = s.p_wide[e, :, columns]
+        value = s.p_wide[pl.ds(pl.multiple_of(e * rows, rows), rows), columns]
         for i in range(1, n):
             value = value + s.p_recv[i, :, columns].astype(F32)
         s.tot[:, columns] = value
@@ -339,7 +345,7 @@
     def g_copy(i, g):
         columns = pl.ds(g * group_cols, group_cols)
         ref = s.att.at[e, :, columns]
-        return remote(ref, ref, s.g_s.at[i, g], s.g_r.at[i, g], ep=up_peer(i))
+        return remote(ref, ref, s.g_s.at[i, g], s.g_r.at[i, g], ep=partner(i))
 
     def attend(g):
         for c in range(g * group_cols // chunk, (g + 1) * group_cols // chunk):
@@ -398,107 +404,93 @@
     piece = min(chunk, half_out)
     pieces = half_out // piece
 
-    def out_part(g, side, c):
-        values = s.att[:, :, g * group_cols : (g + 1) * group_cols].reshape(n * rows, group_cols)
-        columns = pl.ds(pl.multiple_of(side * half_out + c * piece, 128), piece)
-        return dot(values, s.wo[g * group_cols : (g + 1) * group_cols, columns])
-
-    def one_copy(c):
-        columns = pl.ds(c * piece, piece)
-        return remote(
-            s.one_send.at[:, columns], s.one_recv.at[:, columns], s.o_s.at[c], s.o_r.at[c], tp=near
-        )
-
-    for g in range(kv_heads):
-        each(n, lambda i: g_copy(i, g).wait_recv())
-        for k, side in enumerate((1 - b0, b0)):
-            for c in range(pieces):
-                columns = slice(c * piece, (c + 1) * piece)
-                value = out_part(g, side, c)
-                if g > 0:
-                    value = s.acc[k, :, columns] + value
-                if k == 0 and g == kv_heads - 1:
-                    s.one_send[:, columns] = value.astype(BF16)
-                    one_copy(c).start()
-                else:
-                    s.acc[k, :, columns] = value
-
-    def two_copy(c):
-        columns = pl.ds(c * piece, piece)
-        return remote(
-            s.two_send.at[1 - b1, :, :, columns],
-            s.two_recv.at[:, :, columns],
-            s.t_s.at[c],
-            s.t_r.at[c],
-            tp=far,
-        )
-
-    for c in range(pieces):
-        columns = slice(c * piece, (c + 1) * piece)
-        one_copy(c).wait_recv()
-        value = s.acc[1, :, columns] + s.one_recv[:, columns].astype(F32)
-        value = value.reshape(n, rows, piece)
-        for k in range(2):
-            block = value[:, k * half_rows : (k + 1) * half_rows]
-            s.two_wide[k, :, :, columns] = block
-            s.two_send[k, :, :, columns] = block.astype(BF16)
-        two_copy(c).start()
-
-    def place(block, index, c):
+    def place(block, index):
         return (
             pl.ds(pl.multiple_of(lax.div(index, 2) * half_rows, half_rows), half_rows),
             pl.ds(
-                pl.multiple_of(block * out_cols + lax.rem(index, 2) * half_out + c * piece, 128),
-                piece,
+                pl.multiple_of(block * out_cols + lax.rem(index, 2) * half_out, 128), half_out
             ),
         )
 
-    def three_copy(i, c):
-        p = up_peer(i)
+    def one_copy(i):
+        return remote(s.one_send.at[i], s.one_recv.at[i], s.o_s.at[i], s.o_r.at[i], tp=near)
+
+    def two_copy(i):
         return remote(
-            s.three_send.at[p, :, pl.ds(c * piece, piece)],
-            s.out.at[place(e, t, c)],
-            s.h_s.at[i, c],
-            s.h_r.at[i, c],
-            ep=p,
-        )
-
-    def four_copy(i, k, c, index):
-        ref = s.out.at[place(down_peer(i), index, c)]
+            s.two_send.at[i, 1 - b1], s.two_recv.at[i], s.t_s.at[i], s.t_r.at[i], tp=far
+        )
+
+    def three_copy(i):
+        p = partner(i)
         return remote(
-            ref, ref, s.r_s.at[i, k, c], s.r_r.at[i, k, c], tp=far if k == 1 else near
-        )
-
-    def pass_far(i, c):
-        four_copy(i, 1, c, far).wait_recv()
-        four_copy(i, 2, c, far).start()
-
-    for c in range(pieces):
-        columns = slice(c * piece, (c + 1) * piece)
-        two_copy(c).wait_recv()
-        value = s.two_wide[b1, :, :, columns] + s.two_recv[:, :, columns].astype(F32)
-        s.three_send[:, :, columns] = value.astype(BF16)
-        each(n, lambda i: three_copy(i, c).start())
-        s.out[place(e, t, c)] = s.three_send[e, :, columns]
-        four_copy(0, 1, c, t).start()
-        four_copy(0, 0, c, t).start()
-
-    for c in range(pieces):
-
-        def pass_on(i):
-            ref = s.out.at[place(down_peer(i), t, c)]
-            remote(ref, ref, s.h_s.at[i, c], s.h_r.at[i, c], ep=up_peer(i)).wait_recv()
-            four_copy(i, 1, c, t).start()
-            four_copy(i, 0, c, t).start()
-
-        pass_far(0, c)
-        each(n, pass_on)
-        each(n, lambda i: pass_far(i, c))
+            s.three_send.at[i], s.out.at[place(e, t)], s.h_s.at[i], s.h_r.at[i], ep=p
+        )
+
+    def four_copy(i, k, index):
+        ref = s.out.at[place(partner(i), index)]
+        return remote(ref, ref, s.r_s.at[i, k], s.r_r.at[i, k], tp=far if k == 1 else near)
+
+    def project(i, own=False):
+        if not own:
+            for g in range(kv_heads):
+                g_copy(i, g).wait_recv()
+        p = partner(i)
+        values = s.att[p]
+        for k, side in enumerate((1 - b0, b0)):
+            for c in range(pieces):
+                columns = pl.ds(pl.multiple_of(side * half_out + c * piece, 128), piece)
+                value = dot(values, s.wo[:, columns])
+                columns = slice(c * piece, (c + 1) * piece)
+                if k == 0:
+                    s.one_send[i, :, columns] = value.astype(BF16)
+                else:
+                    s.acc[i, :, columns] = value
+            if k == 0:
+                one_copy(i).start()
+
+    def add_near(i, own=False):
+        one_copy(i).wait_recv()
+        value = s.acc[i] + s.one_recv[i].astype(F32)
+        for k in range(2):
+            block = value[k * half_rows : (k + 1) * half_rows]
+            s.two_wide[i, k] = block
+            s.two_send[i, k] = block.astype(BF16)
+        two_copy(i).start()
+
+    def add_far(i, own=False):
+        two_copy(i).wait_recv()
+        value = (s.two_wide[i, b1] + s.two_recv[i].astype(F32)).astype(BF16)
+        if own:
+            s.out[place(e, t)] = value
+        else:
+            s.three_send[i] = value
+            three_copy(i).start()
+
+    def pass_on(i, own=False):
+        if not own:
+            ref = s.out.at[place(partner(i), t)]
+            remote(ref, ref, s.h_s.at[i], s.h_r.at[i], ep=partner(i)).wait_recv()
+        four_copy(i, 1, t).start()
+        four_copy(i, 0, t).start()
+
+    def pass_far(i, own=False):
+        four_copy(i, 1, far).wait_recv()
+        four_copy(i, 2, far).start()
+
+    stages = (project, add_near, add_far, pass_on, pass_far)
+    if n <= UNROLL_PEERS:
+        for step in range(n + len(stages) - 1):
+            for k, stage in enumerate(stages):
+                if 0 <= step - k < n:
+                    stage(step - k, own=step == k)
+    else:
+        for stage in stages:
+            stage(0, own=True)
+            each(n, stage)
 
     def last(i):
-        for c in range(pieces):
-            four_copy(i, 0, c, near).wait_recv()
-            four_copy(i, 2, c, across).wait_recv()
+        four_copy(i, 0, near).wait_recv()
+        four_copy(i, 2, across).wait_recv()
 
     last(0)
     each(n, last)
@@ -513,21 +505,22 @@
             p_copy(i, c).wait_send()
         for g in range(kv_heads):
             g_copy(i, g).wait_send()
-        for c in range(pieces):
-            three_copy(i, c).wait_send()
-            for k in range(3):
-                four_copy(i, k, c, t).wait_send()
+        three_copy(i).wait_send()
         for k in range(3):
             f_copy(i, k, t).wait_send()
 
     each(n, drain)
+
+    def drain_tp(i):
+        one_copy(i).wait_send()
+        two_copy(i).wait_send()
+        for k in range(3):
+            four_copy(i, k, t).wait_send()
+
+    drain_tp(0)
+    each(n, drain_tp)
     for j in range(1, TP):
         s_copy(j).wait_send()
-    for c in range(pieces):
-        for k in range(3):
-            four_copy(0, k, c, t).wait_send()
-        one_copy(c).wait_send()
-        two_copy(c).wait_send()
     final.wait()
 
 
@@ -559,7 +552,6 @@
     group = QUERY_HEADS // KEY_HEADS
     kv_heads = kv_cols // HEAD_SIZE
     chunks = all_cols // 512
-    pieces = half_out // min(512, half_out)
     vmem = pltpu.VMEM
     dma = pltpu.SemaphoreType.DMA
     scratch = dict(
@@ -579,7 +571,7 @@
         ids=vmem((n, 8, 128), jnp.int32),
         sh_send=vmem((slots, 128), F32),
         sh_recv=vmem((TP, slots, 128), F32),
-        p_wide=vmem((n, rows, all_cols), F32),
+        p_wide=vmem((n * rows, all_cols), F32),
         p_send=vmem((n, rows, all_cols), BF16),
         p_recv=vmem((n, rows, all_cols), BF16),
         tot=vmem((rows, all_cols), F32),
@@ -590,11 +582,11 @@
         k3=vmem((rows, group, HEAD_SIZE), F32),
         v3=vmem((rows, group, HEAD_SIZE), F32),
         att=vmem((n, rows, q_cols), BF16),
-        acc=vmem((2, n * rows, half_out), F32),
-        one_send=vmem((n * rows, half_out), BF16),
-        one_recv=vmem((n * rows, half_out), BF16),
-        two_wide=vmem((2, n, rows // 2, half_out), F32),
-        two_send=vmem((2, n, rows // 2, half_out), BF16),
+        acc=vmem((n, rows, half_out), F32),
+        one_send=vmem((n, rows, half_out), BF16),
+        one_recv=vmem((n, rows, half_out), BF16),
+        two_wide=vmem((n, 2, rows // 2, half_out), F32),
+        two_send=vmem((n, 2, rows // 2, half_out), BF16),
         two_recv=vmem((n, rows // 2, half_out), BF16),
         three_send=vmem((n, rows // 2, half_out), BF16),
         out=vmem((rows, width), BF16),
@@ -605,22 +597,22 @@
         m_r=dma((n,)),
         b_s=dma((n,)),
         b_r=dma((n,)),
-        f_s=dma((n, TP)),
-        f_r=dma((n, TP)),
+        f_s=dma((n, 3)),
+        f_r=dma((n, 3)),
         s_s=dma((TP,)),
         s_r=dma((TP,)),
         p_s=dma((n, chunks)),
         p_r=dma((n, chunks)),
         g_s=dma((n, kv_heads)),
         g_r=dma((n, kv_heads)),
-        o_s=dma((pieces,)),
-        o_r=dma((pieces,)),
-        t_s=dma((pieces,)),
-        t_r=dma((pieces,)),
-        h_s=dma((n, pieces)),
-        h_r=dma((n, pieces)),
-        r_s=dma((n, TP, pieces)),
-        r_r=dma((n, TP, pieces)),
+        o_s=dma((n,)),
+        o_r=dma((n,)),
+        t_s=dma((n,)),
+        t_r=dma((n,)),
+        h_s=dma((n,)),
+        h_r=dma((n,)),
+        r_s=dma((n, 3)),
+        r_r=dma((n, 3)),
     )
     operands = [
         "idx_ref",

time: 69.3 us -> 66.3 us (0.957)
  Pallas kernels: 64.2 us -> 61.2 us
    pallas_call x1, Pallas kernels: 64.2 us -> 61.2 us  [local(): pl.pallas_call(functools.partial(body, n, operands + list(scratch)), out_...]
where the time goes in v3:
time: 66.3 us; the launch traced here: 65.4 us
  Pallas kernels  61.2 us (92%)
  local copies, waits for them, and re-layouts  4.2 us (6%)
    pallas_call x1, Pallas kernels, local(): pl.pallas_call(functools.partial(body, n, operands + list(scratch)), out_...  61.2 us
    reshape x1, local copies, waits for them, and re-layouts, local(): return out.reshape(tokens.shape)  2.17 us
    reshape x1, local copies, waits for them, and re-layouts, local(): tokens.reshape(rows, width)  2.03 us

profile of v3, /device:TPU:0, one launch (start us, length us, event | category | flops | bytes accessed | tf_op | source)
XLA Modules:
  0.0 65.4 jit_solution(5245732900572473342)
XLA Ops:
  0.0 2.0 %reshape.6.refs_2_ = bf16[32,8192]{1,0:T(8,128)(2,1)} reshape(bf16[16,2,8192]{2,1,0:T(2,128)(2,1)} %param.11) | data formatting | bytes 1048576 | tf_op jit(solution)/shard_map/reshape | solution.py:645
  2.0 61.2 %sublayer.1 = bf16[32,8192]{1,0:T(8,128)(2,1)} custom-call(s32[16]{0:T(128)} %refs_0_.1, s32[16]{0:T(128)} %refs_1_.1, bf16[32,8192]{1,0:T(8,128)(2,1)} %reshape.6.refs_2_, bf16[2048,2048]{1,0:T(8,128)(2,1)} %refs_3_.1, bf16[2048,256]{1,0:T(8,128)(2,1)} %refs_4_.1, bf16[2048,256]{1,0:T(8,128)(2,1)} %refs_5_.1, bf16[2048,2048]{1,0:T(8,128)(2,1)} %refs_6_.1, ...), custom_call_target="tpu_custom_call" | custom-call | tf_op jit(solution)/shard_map/sublayer/pallas_call | solution.py:631
  63.3 2.2 %reshape.7 = bf16[16,2,8192]{2,1,0:T(2,128)(2,1)} reshape(bf16[32,8192]{1,0:T(8,128)(2,1)} %sublayer.1) | data formatting | bytes 1048576 | tf_op jit(solution)/shard_map/reshape | solution.py:655

commit v4 on v3

--- a/solution.py
+++ b/solution.py
@@ -271,6 +271,8 @@
     loads["wv"].wait()
     row_block = s.x[...].reshape(n * rows, feat)
 
+    paired = n == 4
+
     def p_copy(i, c):
         p = partner(i)
         columns = pl.ds(c * chunk, chunk)
@@ -279,14 +281,27 @@
             s.p_recv.at[i, :, columns],
             s.p_s.at[i, c],
             s.p_r.at[i, c],
-            ep=p,
+            ep=partner(1) if paired and i == 3 else p,
         )
 
     def ship(c, value):
         columns = slice(c * chunk, (c + 1) * chunk)
         s.p_wide[:, columns] = value
         s.p_send[:, :, columns] = value.astype(BF16).reshape(n, rows, chunk)
-        each(n, lambda i: p_copy(i, c).start())
+        if paired:
+            p_copy(1, c).start()
+            p_copy(3, c).start()
+        else:
+            each(n, lambda i: p_copy(i, c).start())
+
+    def ship_far(c):
+        columns = slice(c * chunk, (c + 1) * chunk)
+        p_copy(3, c).wait_recv()
+        p = partner(2)
+        value = s.p_wide[pl.ds(pl.multiple_of(p * rows, rows), rows), columns]
+        value = value + s.p_recv[3, :, columns].astype(F32)
+        s.p_send[p, :, columns] = value.astype(BF16)
+        p_copy(2, c).start()
 
     q_chunks = q_cols // chunk
     kv_chunks = 2 * kv_cols // chunk
@@ -297,6 +312,9 @@
     for c in range(q_chunks):
         columns = slice(c * chunk, (c + 1) * chunk)
         s.p_wide[:, columns] = dot(row_block, s.wq[:, columns])
+    if paired:
+        for c in range(kv_chunks):
+            ship_far(q_chunks + c)
 
     for j in range(1, TP):
         s_copy(j).wait_recv()
@@ -320,12 +338,20 @@
         columns = slice(c * chunk, (c + 1) * chunk)
         delta = dot(spread, up[:, columns]).astype(BF16)
         ship(c, s.p_wide[:, columns] + dot(returning, delta))
+    if paired:
+        for c in range(q_chunks):
+            ship_far(c)
 
     def p_sum(c):
         columns = slice(c * chunk, (c + 1) * chunk)
-        each(n, lambda i: p_copy(i, c).wait_recv())
+        sources = range(1, 3 if paired else n)
+        if paired:
+            for i in sources:
+                p_copy(i, c).wait_recv()
+        else:
+            each(n, lambda i: p_copy(i, c).wait_recv())
         value = s.p_wide[pl.ds(pl.multiple_of(e * rows, rows), rows), columns]
-        for i in range(1, n):
+        for i in sources:
             value = value + s.p_recv[i, :, columns].astype(F32)
         s.tot[:, columns] = value
 
@@ -344,8 +370,16 @@
 
     def g_copy(i, g):
         columns = pl.ds(g * group_cols, group_cols)
+        if paired and i == 3:
+            ref = s.att.at[partner(2), :, columns]
+            return remote(ref, ref, s.g_s.at[i, g], s.g_r.at[i, g], ep=partner(1))
         ref = s.att.at[e, :, columns]
         return remote(ref, ref, s.g_s.at[i, g], s.g_r.at[i, g], ep=partner(i))
+
+    def g_wait(i, g):
+        g_copy(i, g).wait_recv()
+        if paired and i == 2:
+            g_copy(3, g).start()
 
     def attend(g):
         for c in range(g * group_cols // chunk, (g + 1) * group_cols // chunk):
@@ -395,14 +429,14 @@
         for h in range(group):
             at = g * group_cols + h * HEAD_SIZE
             s.att[e, :, at : at + HEAD_SIZE] = s.q3[:, h, :].astype(BF16)
-        each(n, lambda i: g_copy(i, g).start())
-
-    for g in range(kv_heads):
-        attend(g)
-
-    loads["wo"].wait()
-    piece = min(chunk, half_out)
-    pieces = half_out // piece
+        if paired:
+            g_copy(2, g).start()
+            g_copy(1, g).start()
+        else:
+            each(n, lambda i: g_copy(i, g).start())
+
+    piece = min(chunk, out_cols)
+    pieces = out_cols // piece
 
     def place(block, index):
         return (
@@ -412,12 +446,10 @@
             ),
         )
 
-    def one_copy(i):
-        return remote(s.one_send.at[i], s.one_recv.at[i], s.o_s.at[i], s.o_r.at[i], tp=near)
-
-    def two_copy(i):
+    def one_copy(i, j):
+        p = tp_up(j)
         return remote(
-            s.two_send.at[i, 1 - b1], s.two_recv.at[i], s.t_s.at[i], s.t_r.at[i], tp=far
+            s.one_send.at[i, p], s.one_recv.at[i, j], s.o_s.at[i, j], s.o_r.at[i, j], tp=p
         )
 
     def three_copy(i):
@@ -426,40 +458,48 @@
             s.three_send.at[i], s.out.at[place(e, t)], s.h_s.at[i], s.h_r.at[i], ep=p
         )
 
-    def four_copy(i, k, index):
+    def four_copy(i, j, index):
         ref = s.out.at[place(partner(i), index)]
-        return remote(ref, ref, s.r_s.at[i, k], s.r_r.at[i, k], tp=far if k == 1 else near)
+        return remote(ref, ref, s.r_s.at[i, j], s.r_r.at[i, j], tp=tp_up(j))
+
+    def project_head(i, g):
+        values = s.att[partner(i), :, g * group_cols : (g + 1) * group_cols]
+        for c in range(pieces):
+            columns = slice(c * piece, (c + 1) * piece)
+            value = dot(values, s.wo[g * group_cols : (g + 1) * group_cols, columns])
+            if g > 0:
+                value = s.acc[i, :, columns] + value
+            s.acc[i, :, columns] = value
+
+    def project_first(i):
+        for g in range(kv_heads - 1):
+            g_wait(i, g)
+            project_head(i, g)
 
     def project(i, own=False):
         if not own:
-            for g in range(kv_heads):
-                g_copy(i, g).wait_recv()
-        p = partner(i)
-        values = s.att[p]
-        for k, side in enumerate((1 - b0, b0)):
-            for c in range(pieces):
-                columns = pl.ds(pl.multiple_of(side * half_out + c * piece, 128), piece)
-                value = dot(values, s.wo[:, columns])
-                columns = slice(c * piece, (c + 1) * piece)
-                if k == 0:
-                    s.one_send[i, :, columns] = value.astype(BF16)
-                else:
-                    s.acc[i, :, columns] = value
-            if k == 0:
-                one_copy(i).start()
-
-    def add_near(i, own=False):
-        one_copy(i).wait_recv()
-        value = s.acc[i] + s.one_recv[i].astype(F32)
-        for k in range(2):
-            block = value[k * half_rows : (k + 1) * half_rows]
-            s.two_wide[i, k] = block
-            s.two_send[i, k] = block.astype(BF16)
-        two_copy(i).start()
-
-    def add_far(i, own=False):
-        two_copy(i).wait_recv()
-        value = (s.two_wide[i, b1] + s.two_recv[i].astype(F32)).astype(BF16)
+            g_wait(i, kv_heads - 1)
+        project_head(i, kv_heads - 1)
+        for index in range(TP):
+            k, side = index // 2, index % 2
+            s.one_send[i, index] = s.acc[
+                i,
+                k * half_rows : (k + 1) * half_rows,
+                side * half_out : (side + 1) * half_out,
+            ].astype(BF16)
+        for j in range(1, TP):
+            one_copy(i, j).start()
+
+    def add_up(i, own=False):
+        value = s.acc[
+            i,
+            pl.ds(pl.multiple_of(b1 * half_rows, half_rows), half_rows),
+            pl.ds(pl.multiple_of(b0 * half_out, 128), half_out),
+        ]
+        for j in range(1, TP):
+            one_copy(i, j).wait_recv()
+            value = value + s.one_recv[i, j].astype(F32)
+        value = value.astype(BF16)
         if own:
             s.out[place(e, t)] = value
         else:
@@ -470,14 +510,18 @@
         if not own:
             ref = s.out.at[place(partner(i), t)]
             remote(ref, ref, s.h_s.at[i], s.h_r.at[i], ep=partner(i)).wait_recv()
-        four_copy(i, 1, t).start()
-        four_copy(i, 0, t).start()
-
-    def pass_far(i, own=False):
-        four_copy(i, 1, far).wait_recv()
-        four_copy(i, 2, far).start()
-
-    stages = (project, add_near, add_far, pass_on, pass_far)
+        for j in range(1, TP):
+            four_copy(i, j, t).start()
+
+    for g in range(kv_heads):
+        attend(g)
+        if g == 0:
+            loads["wo"].wait()
+        if g < kv_heads - 1:
+            project_head(0, g)
+    each(n, project_first)
+
+    stages = (project, add_up, pass_on)
     if n <= UNROLL_PEERS:
         for step in range(n + len(stages) - 1):
             for k, stage in enumerate(stages):
@@ -489,8 +533,8 @@
             each(n, stage)
 
     def last(i):
-        four_copy(i, 0, near).wait_recv()
-        four_copy(i, 2, across).wait_recv()
+        for j in range(1, TP):
+            four_copy(i, j, tp_down(j)).wait_recv()
 
     last(0)
     each(n, last)
@@ -512,10 +556,9 @@
     each(n, drain)
 
     def drain_tp(i):
-        one_copy(i).wait_send()
-        two_copy(i).wait_send()
-        for k in range(3):
-            four_copy(i, k, t).wait_send()
+        for j in range(1, TP):
+            one_copy(i, j).wait_send()
+            four_copy(i, j, t).wait_send()
 
     drain_tp(0)
     each(n, drain_tp)
@@ -582,12 +625,9 @@
         k3=vmem((rows, group, HEAD_SIZE), F32),
         v3=vmem((rows, group, HEAD_SIZE), F32),
         att=vmem((n, rows, q_cols), BF16),
-        acc=vmem((n, rows, half_out), F32),
-        one_send=vmem((n, rows, half_out), BF16),
-        one_recv=vmem((n, rows, half_out), BF16),
-        two_wide=vmem((n, 2, rows // 2, half_out), F32),
-        two_send=vmem((n, 2, rows // 2, half_out), BF16),
-        two_recv=vmem((n, rows // 2, half_out), BF16),
+        acc=vmem((n, rows, out_cols), F32),
+        one_send=vmem((n, TP, rows // 2, half_out), BF16),
+        one_recv=vmem((n, TP, rows // 2, half_out), BF16),
         three_send=vmem((n, rows // 2, half_out), BF16),
         out=vmem((rows, width), BF16),
         load_sem=dma((9,)),
@@ -605,14 +645,12 @@
         p_r=dma((n, chunks)),
         g_s=dma((n, kv_heads)),
         g_r=dma((n, kv_heads)),
-        o_s=dma((n,)),
-        o_r=dma((n,)),
-        t_s=dma((n,)),
-        t_r=dma((n,)),
+        o_s=dma((n, TP)),
+        o_r=dma((n, TP)),
         h_s=dma((n,)),
         h_r=dma((n,)),
-        r_s=dma((n, 3)),
-        r_r=dma((n, 3)),
+        r_s=dma((n, TP)),
+        r_r=dma((n, TP)),
     )
     operands = [
         "idx_ref",

time: 66.3 us -> 66.2 us (level)
  no operation moved by 1% of the time
where the time goes in v4:
time: 66.2 us; the launch traced here: 66 us
  Pallas kernels  61.7 us (93%)
  local copies, waits for them, and re-layouts  4.2 us (6%)
    pallas_call x1, Pallas kernels, local(): pl.pallas_call(functools.partial(body, n, operands + list(scratch)), out_...  61.7 us
    reshape x1, local copies, waits for them, and re-layouts, local(): return out.reshape(tokens.shape)  2.17 us
    reshape x1, local copies, waits for them, and re-layouts, local(): tokens.reshape(rows, width)  2.03 us

profile of v4, /device:TPU:0, one launch (start us, length us, event | category | flops | bytes accessed | tf_op | source)
XLA Modules:
  0.0 66.0 jit_solution(10965102175537950046)
XLA Ops:
  0.0 2.0 %reshape.6.refs_2_ = bf16[32,8192]{1,0:T(8,128)(2,1)} reshape(bf16[16,2,8192]{2,1,0:T(2,128)(2,1)} %param.11) | data formatting | bytes 1048576 | tf_op jit(solution)/shard_map/reshape | solution.py:683
  2.0 61.7 %sublayer.1 = bf16[32,8192]{1,0:T(8,128)(2,1)} custom-call(s32[16]{0:T(128)} %refs_0_.1, s32[16]{0:T(128)} %refs_1_.1, bf16[32,8192]{1,0:T(8,128)(2,1)} %reshape.6.refs_2_, bf16[2048,2048]{1,0:T(8,128)(2,1)} %refs_3_.1, bf16[2048,256]{1,0:T(8,128)(2,1)} %refs_4_.1, bf16[2048,256]{1,0:T(8,128)(2,1)} %refs_5_.1, bf16[2048,2048]{1,0:T(8,128)(2,1)} %refs_6_.1, ...), custom_call_target="tpu_custom_call" | custom-call | tf_op jit(solution)/shard_map/sublayer/pallas_call | solution.py:669
  63.8 2.2 %reshape.7 = bf16[16,2,8192]{2,1,0:T(2,128)(2,1)} reshape(bf16[32,8192]{1,0:T(8,128)(2,1)} %sublayer.1) | data formatting | bytes 1048576 | tf_op jit(solution)/shard_map/reshape | solution.py:693

commit v5 on v4

--- a/solution.py
+++ b/solution.py
@@ -222,6 +222,57 @@
 
     each(n, forward)
     each(n, forward_far)
+
+    def f_in(i):
+        f_copy(i, 0, near).wait_recv()
+        f_copy(i, 2, across).wait_recv()
+
+    each(n, f_in)
+    loads["wk"].wait()
+    loads["wv"].wait()
+    row_block = s.x[...].reshape(n * rows, feat)
+
+    paired = n == 4
+
+    def p_copy(i, c):
+        p = partner(i)
+        columns = pl.ds(c * chunk, chunk)
+        return remote(
+            s.p_send.at[p, :, columns],
+            s.p_recv.at[i, :, columns],
+            s.p_s.at[i, c],
+            s.p_r.at[i, c],
+            ep=partner(1) if paired and i == 3 else p,
+        )
+
+    def ship(c, value):
+        columns = slice(c * chunk, (c + 1) * chunk)
+        s.p_wide[:, columns] = value
+        s.p_send[:, :, columns] = value.astype(BF16).reshape(n, rows, chunk)
+        if paired:
+            p_copy(1, c).start()
+            p_copy(3, c).start()
+        else:
+            each(n, lambda i: p_copy(i, c).start())
+
+    def ship_far(c):
+        columns = slice(c * chunk, (c + 1) * chunk)
+        p_copy(3, c).wait_recv()
+        p = partner(2)
+        value = s.p_wide[pl.ds(pl.multiple_of(p * rows, rows), rows), columns]
+        value = value + s.p_recv[3, :, columns].astype(F32)
+        s.p_send[p, :, columns] = value.astype(BF16)
+        p_copy(2, c).start()
+
+    q_chunks = q_cols // chunk
+    kv_chunks = 2 * kv_cols // chunk
+    for c in range(kv_chunks):
+        ship(q_chunks + c, dot(row_block, s.wkv[:, c * chunk : (c + 1) * chunk]))
+
+    loads["wq"].wait()
+    for c in range(q_chunks):
+        columns = slice(c * chunk, (c + 1) * chunk)
+        s.p_wide[:, columns] = dot(row_block, s.wq[:, columns])
 
     def b_in(i):
         m_copy(i).wait_recv()
@@ -262,56 +313,6 @@
     for j in range(1, TP):
         s_copy(j).start()
 
-    def f_in(i):
-        f_copy(i, 0, near).wait_recv()
-        f_copy(i, 2, across).wait_recv()
-
-    each(n, f_in)
-    loads["wk"].wait()
-    loads["wv"].wait()
-    row_block = s.x[...].reshape(n * rows, feat)
-
-    paired = n == 4
-
-    def p_copy(i, c):
-        p = partner(i)
-        columns = pl.ds(c * chunk, chunk)
-        return remote(
-            s.p_send.at[p, :, columns],
-            s.p_recv.at[i, :, columns],
-            s.p_s.at[i, c],
-            s.p_r.at[i, c],
-            ep=partner(1) if paired and i == 3 else p,
-        )
-
-    def ship(c, value):
-        columns = slice(c * chunk, (c + 1) * chunk)
-        s.p_wide[:, columns] = value
-        s.p_send[:, :, columns] = value.astype(BF16).reshape(n, rows, chunk)
-        if paired:
-            p_copy(1, c).start()
-            p_copy(3, c).start()
-        else:
-            each(n, lambda i: p_copy(i, c).start())
-
-    def ship_far(c):
-        columns = slice(c * chunk, (c + 1) * chunk)
-        p_copy(3, c).wait_recv()
-        p = partner(2)
-        value = s.p_wide[pl.ds(pl.multiple_of(p * rows, rows), rows), columns]
-        value = value + s.p_recv[3, :, columns].astype(F32)
-        s.p_send[p, :, columns] = value.astype(BF16)
-        p_copy(2, c).start()
-
-    q_chunks = q_cols // chunk
-    kv_chunks = 2 * kv_cols // chunk
-    for c in range(kv_chunks):
-        ship(q_chunks + c, dot(row_block, s.wkv[:, c * chunk : (c + 1) * chunk]))
-
-    loads["wq"].wait()
-    for c in range(q_chunks):
-        columns = slice(c * chunk, (c + 1) * chunk)
-        s.p_wide[:, columns] = dot(row_block, s.wq[:, columns])
     if paired:
         for c in range(kv_chunks):
             ship_far(q_chunks + c)
@@ -519,18 +520,29 @@
             loads["wo"].wait()
         if g < kv_heads - 1:
             project_head(0, g)
-    each(n, project_first)
-
-    stages = (project, add_up, pass_on)
-    if n <= UNROLL_PEERS:
-        for step in range(n + len(stages) - 1):
-            for k, stage in enumerate(stages):
-                if 0 <= step - k < n:
-                    stage(step - k, own=step == k)
+    project(0, own=True)
+    if paired:
+        project_first(2)
+        project_first(1)
+        add_up(0, own=True)
+        project_first(3)
+        project(2)
+        pass_on(0, own=True)
+        project(1)
+        add_up(2)
+        project(3)
+        add_up(1)
+        pass_on(2)
+        add_up(3)
+        pass_on(1)
+        pass_on(3)
     else:
-        for stage in stages:
-            stage(0, own=True)
-            each(n, stage)
+        each(n, project_first)
+        each(n, project)
+        add_up(0, own=True)
+        each(n, add_up)
+        pass_on(0, own=True)
+        each(n, pass_on)
 
     def last(i):
         for j in range(1, TP):

time: 66.2 us -> 63.6 us (0.961)
  Pallas kernels: 61.7 us -> 59.1 us
    pallas_call x1, Pallas kernels: 61.7 us -> 59.1 us  [local(): pl.pallas_call(functools.partial(body, n, operands + list(scratch)), out_...]
where the time goes in v5:
time: 63.6 us; the launch traced here: 63.3 us
  Pallas kernels  59.1 us (93%)
  local copies, waits for them, and re-layouts  4.2 us (7%)
    pallas_call x1, Pallas kernels, local(): pl.pallas_call(functools.partial(body, n, operands + list(scratch)), out_...  59.1 us
    reshape x1, local copies, waits for them, and re-layouts, local(): return out.reshape(tokens.shape)  2.17 us
    reshape x1, local copies, waits for them, and re-layouts, local(): tokens.reshape(rows, width)  2.03 us

profile of v5, /device:TPU:0, one launch (start us, length us, event | category | flops | bytes accessed | tf_op | source)
XLA Modules:
  0.0 63.3 jit_solution(6905231366630105716)
XLA Ops:
  0.0 2.0 %reshape.6.refs_2_ = bf16[32,8192]{1,0:T(8,128)(2,1)} reshape(bf16[16,2,8192]{2,1,0:T(2,128)(2,1)} %param.11) | data formatting | bytes 1048576 | tf_op jit(solution)/shard_map/reshape | solution.py:695
  2.0 59.1 %sublayer.1 = bf16[32,8192]{1,0:T(8,128)(2,1)} custom-call(s32[16]{0:T(128)} %refs_0_.1, s32[16]{0:T(128)} %refs_1_.1, bf16[32,8192]{1,0:T(8,128)(2,1)} %reshape.6.refs_2_, bf16[2048,2048]{1,0:T(8,128)(2,1)} %refs_3_.1, bf16[2048,256]{1,0:T(8,128)(2,1)} %refs_4_.1, bf16[2048,256]{1,0:T(8,128)(2,1)} %refs_5_.1, bf16[2048,2048]{1,0:T(8,128)(2,1)} %refs_6_.1, ...), custom_call_target="tpu_custom_call" | custom-call | tf_op jit(solution)/shard_map/sublayer/pallas_call | solution.py:681
  61.2 2.2 %reshape.7 = bf16[16,2,8192]{2,1,0:T(2,128)(2,1)} reshape(bf16[32,8192]{1,0:T(8,128)(2,1)} %sublayer.1) | data formatting | bytes 1048576 | tf_op jit(solution)/shard_map/reshape | solution.py:705

commit v6 on v5

--- a/solution.py
+++ b/solution.py
@@ -529,8 +529,8 @@
         project(2)
         pass_on(0, own=True)
         project(1)
+        project(3)
         add_up(2)
-        project(3)
         add_up(1)
         pass_on(2)
         add_up(3)

time: 63.6 us -> 63.3 us (level)
  no operation moved by 1% of the time
where the time goes in v6:
time: 63.3 us; the launch traced here: 63.1 us
  Pallas kernels  58.9 us (93%)
  local copies, waits for them, and re-layouts  4.2 us (7%)
    pallas_call x1, Pallas kernels, local(): pl.pallas_call(functools.partial(body, n, operands + list(scratch)), out_...  58.9 us
    reshape x1, local copies, waits for them, and re-layouts, local(): return out.reshape(tokens.shape)  2.17 us
    reshape x1, local copies, waits for them, and re-layouts, local(): tokens.reshape(rows, width)  2.03 us

profile of v6, /device:TPU:0, one launch (start us, length us, event | category | flops | bytes accessed | tf_op | source)
XLA Modules:
  0.0 63.1 jit_solution(12504611421627509452)
XLA Ops:
  0.0 2.0 %reshape.6.refs_2_ = bf16[32,8192]{1,0:T(8,128)(2,1)} reshape(bf16[16,2,8192]{2,1,0:T(2,128)(2,1)} %param.11) | data formatting | bytes 1048576 | tf_op jit(solution)/shard_map/reshape | solution.py:695
  2.0 58.9 %sublayer.1 = bf16[32,8192]{1,0:T(8,128)(2,1)} custom-call(s32[16]{0:T(128)} %refs_0_.1, s32[16]{0:T(128)} %refs_1_.1, bf16[32,8192]{1,0:T(8,128)(2,1)} %reshape.6.refs_2_, bf16[2048,2048]{1,0:T(8,128)(2,1)} %refs_3_.1, bf16[2048,256]{1,0:T(8,128)(2,1)} %refs_4_.1, bf16[2048,256]{1,0:T(8,128)(2,1)} %refs_5_.1, bf16[2048,2048]{1,0:T(8,128)(2,1)} %refs_6_.1, ...), custom_call_target="tpu_custom_call" | custom-call | tf_op jit(solution)/shard_map/sublayer/pallas_call | solution.py:681
  60.9 2.2 %reshape.7 = bf16[16,2,8192]{2,1,0:T(2,128)(2,1)} reshape(bf16[32,8192]{1,0:T(8,128)(2,1)} %sublayer.1) | data formatting | bytes 1048576 | tf_op jit(solution)/shard_map/reshape | solution.py:705
